TPU v7x, 512 devices: a whole 4x8x8 slice. The times are simulated.
512 devices in a mesh: dp: 4 (over z_lo, core), fsdp: 32 (over z_hi, y), seq: 4 (over x).
Axes of the slice: x: 4, y: 8, z: 8 (z_hi: 4, z_lo: 2; z = z_hi * 2 + z_lo), core: 2. Of those that a mesh axis runs over, the one named last changes fastest.
Arguments:
- layer_input: bfloat16 [256, 256, 8192], P(('dp', 'fsdp'), 'seq'), may hold values from -6 to 6
- next_token_rows: bfloat16 [256, 256, 8192], P(('dp', 'fsdp'), 'seq'), may hold values from -0.0625 to 0.0625
- response_length: int32 [256], P(('dp', 'fsdp')), may hold values from 32 to 256, as said below
- input_norm_scale: float32 [8192], replicated, may hold values from 0.1 to 1.9
- query_weight: bfloat16 [8192, 128], P('fsdp'), may hold values from -0.0625 to 0.0625
- key_weight: bfloat16 [8192, 128], P('fsdp'), may hold values from -0.0625 to 0.0625
- value_weight: bfloat16 [8192, 128], P('fsdp'), may hold values from -0.0625 to 0.0625
- output_projection_weight: bfloat16 [8192, 128], P('fsdp'), may hold values from -0.5 to 0.5
- adapter_down_weight: bfloat16 [8192, 64], P('fsdp'), may hold values from -0.0625 to 0.0625
- adapter_up_weight: bfloat16 [64, 128], replicated, may hold values from -0.75 to 0.75
Outputs:
- dpo_loss: float32 [], replicated
- grad_down: float32 [8192, 64], P(('fsdp', 'seq'))
- grad_up: float32 [64, 128], replicated
Inputs may be any that keep to these rules, and one draw needn't show every extreme that they name: `response_length`: every draw has a sequence with the longest and one with the shortest response.
All inputs are finite; a program needn't handle non-finite values.
Results may differ from a plain program's by a relative error of at most 0.013.
Values may be sent and summed in bfloat16 or wider, within the bound.
A program may use at most 64 MiB of HBM per device.

v0:
```python
import math

import jax
import jax.numpy as jnp
from jax import lax
from jax.sharding import PartitionSpec as P

theta_base = 500000.0
beta_dpo = 0.1
eps_norm = 1e-05


def rotate(field, position):
    half_size = field.shape[-1] // 2
    frequency = theta_base ** (-2.0 * jnp.arange(half_size, dtype=jnp.float32) / field.shape[-1])
    angles = position.astype(jnp.float32)[:, None] * frequency[None, :]
    cosine = jnp.cos(angles)
    sine_wave = jnp.sin(angles)
    first_half = field[..., :half_size]
    second_half = field[..., half_size:]
    return jnp.concatenate(
        [
            first_half * cosine - second_half * sine_wave,
            second_half * cosine + first_half * sine_wave,
        ],
        axis=-1,
    )


def normed(rows, input_norm_scale):
    wide_rows = rows.astype(jnp.float32)
    adapter_scale = lax.rsqrt(jnp.mean(wide_rows * wide_rows, axis=-1, keepdims=True) + eps_norm)
    return (wide_rows * adapter_scale * input_norm_scale).astype(jnp.bfloat16)


def on_device(
    layer_input,
    next_token_rows,
    response_length,
    input_norm_scale,
    query_weight,
    key_weight,
    value_weight,
    output_projection_weight,
    adapter_down_weight,
    adapter_up_weight,
):
    members, segment, model_width = layer_input.shape
    head_size = query_weight.shape[1]
    groups = lax.axis_size("seq")
    length = segment * groups
    tokens = members * segment
    flat_rows = layer_input.reshape(tokens, model_width)
    normalized_rows = normed(flat_rows, input_norm_scale)
    position = lax.axis_index("seq") * segment + jnp.arange(segment, dtype=jnp.int32)
    pieces = (
        lax.all_gather(query_weight, "fsdp", axis=0, tiled=True),
        lax.all_gather(key_weight, "fsdp", axis=0, tiled=True),
        lax.all_gather(value_weight, "fsdp", axis=0, tiled=True),
        lax.all_gather(adapter_down_weight, "fsdp", axis=0, tiled=True),
    )
    columns = normalized_rows
    query_raw, key_raw, frozen_value, adapter_raw = tuple(
        (
            jnp.dot(columns, weight_rows, preferred_element_type=jnp.float32)
            for weight_rows in pieces
        )
    )
    query = rotate(query_raw.reshape(members, segment, head_size), position).astype(jnp.bfloat16)
    own_keys = rotate(key_raw.reshape(members, segment, head_size), position).astype(jnp.bfloat16)
    adapter_input = adapter_raw.astype(jnp.bfloat16)
    value_ref = frozen_value.astype(jnp.bfloat16).reshape(members, segment, head_size)
    policy_value = (
        (
            frozen_value
            + jnp.dot(adapter_input, adapter_up_weight, preferred_element_type=jnp.float32)
        )
        .astype(jnp.bfloat16)
        .reshape(members, segment, head_size)
    )
    all_keys, values_ref, values_pol = (
        lax.all_gather(own_keys, "seq", axis=1, tiled=True),
        lax.all_gather(value_ref, "seq", axis=1, tiled=True),
        lax.all_gather(policy_value, "seq", axis=1, tiled=True),
    )
    scores = jnp.einsum(
        "sqh,skh->sqk", query, all_keys, preferred_element_type=jnp.float32
    ) / math.sqrt(head_size)
    allowed = jnp.arange(length, dtype=jnp.int32)[None, :] <= position[:, None]
    scores = jnp.where(allowed[None], scores, -jnp.inf)
    attention = jax.nn.softmax(scores, axis=-1).astype(jnp.bfloat16)
    values = jnp.stack([values_ref, values_pol])
    mixed_heads = jnp.einsum(
        "sqk,mskh->msqh", attention, values, preferred_element_type=jnp.float32
    ).astype(jnp.bfloat16)
    stacked = mixed_heads.reshape(2 * tokens, head_size)
    projected = jnp.dot(
        stacked,
        lax.all_gather(output_projection_weight, "fsdp", axis=0, tiled=True).T,
        preferred_element_type=jnp.float32,
    )
    resid = projected.reshape(2, tokens, model_width) + flat_rows.astype(jnp.float32)[None]
    inverse = lax.rsqrt(jnp.mean(resid * resid, axis=-1, keepdims=True) + eps_norm)
    unit_rows = resid * inverse
    target = next_token_rows.reshape(tokens, model_width).astype(jnp.float32)
    logits = jnp.sum(unit_rows * target[None], axis=-1).reshape(2, members, segment)
    response = (position[None, :] >= length - response_length[:, None]).astype(jnp.float32)
    partial_scores = jnp.sum(logits * response[None], axis=-1)
    totals = lax.psum(partial_scores, "seq")
    model_gap = totals[1] - totals[0]
    margin = beta_dpo * (model_gap[0] - model_gap[1])
    pair_count = lax.axis_size("dp") * lax.axis_size("fsdp")
    dpo_loss = lax.psum(jax.nn.softplus(-margin), ("dp", "fsdp")) / pair_count
    chosen_weight = -beta_dpo * jax.nn.sigmoid(-margin) / pair_count
    adapter_scale = jnp.stack([chosen_weight, -chosen_weight])
    logit_grad = (adapter_scale[:, None] * response).reshape(tokens, 1)
    unit_grad = logit_grad * target
    unit_pol = unit_rows[1]
    resid_grad = inverse[1] * (
        unit_grad - unit_pol * jnp.mean(unit_grad * unit_pol, axis=-1, keepdims=True)
    )
    resid_rows = resid_grad.astype(jnp.bfloat16)
    columns = resid_rows
    head_raw = jnp.dot(
        columns,
        lax.all_gather(output_projection_weight, "fsdp", axis=0, tiled=True),
        preferred_element_type=jnp.float32,
    )
    head_grad = head_raw.astype(jnp.bfloat16).reshape(members, segment, head_size)
    value_terms = jnp.einsum(
        "sqk,sqh->skh", attention, head_grad, preferred_element_type=jnp.float32
    )
    value_grad = lax.psum_scatter(value_terms, "seq", scatter_dimension=1, tiled=True)
    value_matrix_rows = value_grad.reshape(tokens, head_size).astype(jnp.bfloat16)
    up_product = jnp.dot(adapter_input.T, value_matrix_rows, preferred_element_type=jnp.float32)
    adapter_gradient = jnp.dot(
        value_matrix_rows, adapter_up_weight.T, preferred_element_type=jnp.float32
    ).astype(jnp.bfloat16)
    down_product = jnp.dot(normalized_rows.T, adapter_gradient, preferred_element_type=jnp.float32)
    grad_up = lax.psum(up_product, ("dp", "fsdp", "seq"))
    own_shard = lax.psum_scatter(down_product, ("fsdp", "seq"), scatter_dimension=0, tiled=True)
    grad_down = lax.psum(own_shard, "dp")
    return (dpo_loss, grad_down, grad_up)


def solution(mesh):
    return jax.shard_map(
        on_device,
        mesh=mesh,
        in_specs=(
            P(("dp", "fsdp"), "seq", None),
            P(("dp", "fsdp"), "seq", None),
            P(("dp", "fsdp")),
            P(),
            P("fsdp", None),
            P("fsdp", None),
            P("fsdp", None),
            P("fsdp", None),
            P("fsdp", None),
            P(),
        ),
        out_specs=(P(), P(("fsdp", "seq"), None), P()),
        check_vma=False,
    )
```

profile of v0, /device:TPU:1, one launch (start us, length us, event | category | flops | bytes accessed | tf_op | source)
XLA Modules:
  0.0 1282.8 jit_solution(9815376689410133360)
XLA Ops:
  13.1 3.9 convert.28
  17.1 2.4 convert.18
  20.4 74.6 %all-gather.8.cloned.1.call-done = bf16[8192,64]{0,1:T(8,128)(2,1)} async-done(((bf16[256,64]{0,1:T(8,128)(2,1)}), bf16[8192,64]{0,1:T(8,128)(2,1)}) %all-gather.8.cloned.1.call-update) | async-done | bytes 1048592 | tf_op jit(solution)/shard_map/all_gather | solution.py:60
  97.1 83.9 %all-gather.12.cloned.1.call-done = bf16[8192,128]{1,0:T(8,128)(2,1)} async-done(((bf16[256,128]{1,0:T(8,128)(2,1)}), bf16[8192,128]{1,0:T(8,128)(2,1)}) %all-gather.12.cloned.1.call-update) | async-done | bytes 2097168 | tf_op jit(solution)/shard_map/all_gather | solution.py:58
  181.0 3.0 fusion.2
  184.0 83.2 %all-gather.10.cloned.1.call-done = bf16[8192,128]{1,0:T(8,128)(2,1)} async-done(((bf16[256,128]{1,0:T(8,128)(2,1)}), bf16[8192,128]{1,0:T(8,128)(2,1)}) %all-gather.10.cloned.1.call-update) | async-done | bytes 2097168 | tf_op jit(solution)/shard_map/all_gather | solution.py:57
  267.2 3.0 fusion.4
  270.5 9.8 all_gather.31
  280.3 72.9 %all-gather.6.cloned.1.call-done = bf16[8192,128]{1,0:T(8,128)(2,1)} async-done(((bf16[256,128]{1,0:T(8,128)(2,1)}), bf16[8192,128]{1,0:T(8,128)(2,1)}) %all-gather.6.cloned.1.call-update) | async-done | bytes 2097168 | tf_op jit(solution)/shard_map/all_gather | solution.py:59
  353.2 2.3 fusion.26
  355.7 9.8 all_gather.28
  365.6 9.9 all_gather.26
  376.2 63.0 %all-gather.14.cloned.1.call-done = bf16[8192,128]{1,0:T(8,128)(2,1)} async-done(((bf16[256,128]{1,0:T(8,128)(2,1)}), bf16[8192,128]{1,0:T(8,128)(2,1)}) %all-gather.14.cloned.1.call-update) | async-done | bytes 2097168 | tf_op jit(solution)/shard_map/all_gather | solution.py:99
  439.3 4.2 multiply_reduce_fusion.1
  443.5 6.7 multiply_reduce_fusion
  450.3 8.8 psum.28
  461.4 3.7 multiply_reduce_fusion.2
  465.5 3.4 fusion.12
  470.0 22.3 %reduce-scatter.3.cloned.1.call-done = f32[2,64,128]{2,1,0:T(8,128)} async-done(((f32[2,256,128]{2,1,0:T(8,128)}), f32[2,64,128]{2,1,0:T(8,128)}) %reduce-scatter.3.cloned.1.call-update) | async-done | bytes 65552 | tf_op jit(solution)/shard_map/reduce_scatter | solution.py:133
  493.2 2.8 fusion.13
  496.1 291.4 %psum.29 = f32[]{:T(128)} all-reduce(f32[]{:T(128)S(6)} %select_n.9), channel_id=1, replica_groups=mesh['dp'=4,'fsdp'=32,'seq'=4] {'dp','fsdp'}, use_global_device_ids=true, to_apply=%region_7.8 | all-reduce | flops 1 | bytes 8 | tf_op jit(solution)/shard_map/psum | solution.py:113
  788.2 120.0 %psum.31 = f32[64,128]{1,0:T(8,128)} all-reduce(f32[64,128]{1,0:T(8,128)S(1)} %fusion.28), channel_id=1, replica_groups=mesh['dp'=4,'fsdp'=32,'seq'=4] {'dp','fsdp','seq'}, use_global_device_ids=true, to_apply=%region_12.13 | all-reduce | flops 8192 | bytes 65536 | tf_op jit(solution)/shard_map/psum | solution.py:140
  908.2 250.2 %reduce-scatter.5.cloned.1.call-done = f32[64,64]{1,0:T(8,128)} async-done(((f32[8192,64]{1,0:T(8,128)}), f32[64,64]{1,0:T(8,128)}) %reduce-scatter.5.cloned.1.call-update) | async-done | bytes 16400 | tf_op jit(solution)/shard_map/reduce_scatter | solution.py:141
  1158.4 116.4 %psum.30 = f32[64,64]{1,0:T(8,128)} all-reduce(f32[64,64]{1,0:T(8,128)} %reduce-scatter.5.cloned.1.call-done), channel_id=1, replica_groups=mesh['dp'=4,'fsdp'=32,'seq'=4] {'dp'}, use_global_device_ids=true, to_apply=%region_11.12 | all-reduce | flops 4096 | bytes 32768 | tf_op jit(solution)/shard_map/psum | solution.py:142
  (64 shorter events, 13.4 us)
Async XLA Ops:
  7.2 348.4 %copy-start = (bf16[64,128]{1,0:T(8,128)(2,1)S(1)}, bf16[64,128]{1,0:T(8,128)(2,1)}, u32[]{:S(2)}) copy-start(bf16[64,128]{1,0:T(8,128)(2,1)} %param.19) | copy-start | bytes 49156
  7.2 87.8 %all-gather.8.cloned.1.call-start = ((), (), s32[]{:S(2)}) async-start(), calls=%async_computation.3 | async-start | bytes 1081344 | tf_op jit(solution)/shard_map/all_gather | solution.py:60
  7.9 173.1 %all-gather.12.cloned.1.call-start = ((), (), s32[]{:S(2)}) async-start(), calls=%async_computation.5 | async-start | bytes 2162688 | tf_op jit(solution)/shard_map/all_gather | solution.py:58
  8.7 258.5 %all-gather.10.cloned.1.call-start = ((), (), s32[]{:S(2)}) async-start(), calls=%async_computation.4 | async-start | bytes 2162688 | tf_op jit(solution)/shard_map/all_gather | solution.py:57
  9.4 343.8 %all-gather.6.cloned.1.call-start = ((), (), s32[]{:S(2)}) async-start(), calls=%async_computation.2 | async-start | bytes 2162688 | tf_op jit(solution)/shard_map/all_gather | solution.py:59
  10.0 429.3 %all-gather.14.cloned.1.call-start = ((), (), s32[]{:S(2)}) async-start(), calls=%async_computation.6 | async-start | bytes 2162688 | tf_op jit(solution)/shard_map/all_gather | solution.py:99
  10.6 481.8 %reduce-scatter.3.cloned.1.call-start = ((), (), s32[]{:S(2)}) async-start(), calls=%async_computation.7 | async-start | bytes 327680 | tf_op jit(solution)/shard_map/reduce_scatter | solution.py:133
  10.7 6.4 copy-start.4
  17.0 2.4 copy-start.8
  17.1 2.7 copy-start.3
  17.1 2.7 copy-start.7
  20.3 332.9 %copy-start.1 = (bf16[128,8192]{1,0:T(8,128)(2,1)}, bf16[128,8192]{1,0:T(8,128)(2,1)S(1)}, u32[]{:S(2)}) copy-start(bf16[128,8192]{1,0:T(8,128)(2,1)S(1)} %multiply_convert_fusion.2) | copy-start | bytes 6291460
  461.4 3.7 copy-start.5
  461.4 4.1 copy-start.6
  465.5 27.7 %copy-start.2 = (bf16[128,8192]{1,0:T(8,128)(2,1)S(1)}, bf16[128,8192]{1,0:T(8,128)(2,1)}, u32[]{:S(2)}) copy-start(bf16[128,8192]{1,0:T(8,128)(2,1)} %copy-done.1) | copy-start | bytes 6291460
  470.0 688.4 %reduce-scatter.5.cloned.1.call-start = ((), (), s32[]{:S(2)}) async-start(), calls=%async_computation.8 | async-start | bytes 4227072 | tf_op jit(solution)/shard_map/reduce_scatter | solution.py:141
Sparse Core Ops, SparseCore 0:
  11.1 83.8 all-gather.7
  98.2 82.8 all-gather.11
  184.2 82.9 all-gather.9
  270.2 82.9 all-gather.5
  356.3 82.9 all-gather.13
  470.1 22.1 reduce-scatter.2
  496.1 662.2 reduce-scatter.4
where the time goes:
time: 1280 us
  waiting for transfers between devices  653 us (51%)
  blocking collectives  566 us (44%)
  matrix products  22.7 us (2%)
  other arithmetic  21.4 us (2%)
  between operations  17.6 us (1%)
    psum x1, blocking collectives, on_device(): dpo_loss = lax.psum(jax.nn.softplus(-margin), ('dp', 'fsdp')) / pair_count  291 us
    reduce_scatter x1, waiting for transfers between devices, on_device(): lax.psum_scatter(down_product, ('fsdp', 'seq'), scatter_dimension=0, tile...  250 us
    psum x1, blocking collectives, on_device(): grad_up = lax.psum(up_product, ('dp', 'fsdp', 'seq'))  120 us
    psum x1, blocking collectives, on_device(): grad_down = lax.psum(own_shard, 'dp')  116 us
    all_gather x1, waiting for transfers between devices, on_device(): lax.all_gather(key_weight, 'fsdp', axis=0, tiled=True)  83.9 us
    all_gather x1, waiting for transfers between devices, on_device(): lax.all_gather(query_weight, 'fsdp', axis=0, tiled=True)  83.2 us
    all_gather x1, waiting for transfers between devices, on_device(): lax.all_gather(adapter_down_weight, 'fsdp', axis=0, tiled=True)  74.6 us
    all_gather x1, waiting for transfers between devices, on_device(): lax.all_gather(value_weight, 'fsdp', axis=0, tiled=True)  72.9 us
  transfers between devices with their start and end apart: 7, of which 7 were waited for; matrix products, arithmetic and copies ran while one was open for 2% of the time, Pallas kernels for 0%

commit v1 on v0

v1 whole, which is shorter than its diff:
```python
import math

import jax
import jax.numpy as jnp
from jax import lax
from jax.experimental import pallas as pl
from jax.experimental.pallas import tpu as pltpu
from jax.sharding import PartitionSpec as P

theta_base = 500000.0
beta_dpo = 0.1
eps_norm = 1e-05

LAG = 2
ROUNDS = [[None, None, (0, 0, 0), (0, 0, 1), (0, 0, 0), None], [None, None, (0, 0, 1), (0, 0, 0), (0, 0, 1), None], [None, None, (7, 0, 0), (1, 0, 1), (1, 0, 1), (0, 1, 0)], [None, None, (7, 0, 1), (1, 0, 0), (7, 0, 1), (0, 1, 1)], [None, (1, 1, 1), (6, 0, 0), (2, 0, 1), (0, 2, 0), (1, 1, 1)], [None, (7, 1, 1), (6, 0, 1), (2, 0, 0), (0, 2, 1), (7, 1, 1)], [(1, 2, 1), None, (0, 3, 0), (1, 2, 1), (3, 0, 1), None], [(7, 2, 1), None, (7, 2, 1), (0, 3, 0), (5, 0, 1), None], [(2, 2, 1), (3, 1, 1), (7, 3, 0), (3, 1, 1), (2, 2, 1), (3, 1, 1)], [(5, 1, 1), (6, 2, 1), (5, 0, 1), (1, 3, 0), (6, 2, 1), (5, 1, 1)], [(4, 1, 1), (3, 2, 1), (6, 3, 0), (3, 0, 0), (3, 2, 1), (4, 1, 1)], [(7, 3, 0), (5, 2, 1), (7, 1, 0), (2, 3, 0), (5, 2, 1), (2, 2, 1)], [(4, 2, 1), (1, 3, 0), (5, 3, 0), (1, 1, 0), (4, 2, 1), (6, 2, 1)]]


def arrives(way, block):
    dy, pair, half = block
    if way < 2:
        return (dy, pair, 1 - half)
    if way == 2:
        return ((dy - 1) % 8, pair, half)
    if way == 3:
        return ((dy + 1) % 8, pair, half)
    if way == 4:
        return (dy, (1, 0, 3, 2)[pair], half)
    return (dy, (0, 2, 1, 3)[pair], half)


def dot(a, b):
    return jnp.dot(a, b, preferred_element_type=jnp.float32)


def dot_general(a, b, ca, cb):
    return lax.dot_general(a, b, (((ca,), (cb,)), ((), ())), preferred_element_type=jnp.float32)


def kernel(
    x_hbm, t_hbm, rlen, scale, wq, wk, wv, wo, wd, aup,
    loss_ref, gdown_ref, gup_ref,
    xs, ts, nx, W, acc, kv, att, vgs, vgr, vgo, mgs, mgr,
    dkeep, dsend, drecv, s1, r1y, r1z, s2y, s2z, r2y, r2z, s3, r3, s4, r4,
    us, ur, uxs, uxr, uys, uyr, uzs, uzr, ucs, ucr, ues, uer, stat,
    in_sem, ag_s, ag_r, cc_s, cc_r, kv_s, kv_r, vg_s, vg_r, mg_s, mg_r, dc_s, dc_r,
    y1_s, y1_r, z1_s, z1_r, y2_s, y2_r, z2_s, z2_r, x3_s, x3_r, c4_s, c4_r,
    uc_s, uc_r, ux_s, ux_r, uy_s, uy_r, uz_s, uz_r, ue_s, ue_r,
):
    f32, bf16 = jnp.float32, jnp.bfloat16
    dp, f, x = lax.axis_index("dp"), lax.axis_index("fsdp"), lax.axis_index("seq")
    h, y, zl, c = f // 8, f % 8, dp // 2, dp % 2
    z = h * 2 + zl

    def dev(xx, yy, zz, cc):
        return {"dp": (zz % 2) * 2 + cc, "fsdp": (zz // 2) * 8 + yy, "seq": xx}

    outer = (z + 7 + 2 * zl) % 8
    inner = (z + 1 + 6 * zl) % 8
    sib = dev(x, y, z, 1 - c)
    ways = [
        dev((x + 1) % 4, y, z, c),
        dev((x + 3) % 4, y, z, c),
        dev(x, (y + 1) % 8, z, c),
        dev(x, (y + 7) % 8, z, c),
        dev(x, y, outer, c),
        dev(x, y, inner, c),
    ]

    def remote(src, dst, ss, rs, to):
        return pltpu.make_async_remote_copy(src_ref=src, dst_ref=dst, send_sem=ss, recv_sem=rs, device_id=to)

    in_x = pltpu.make_async_copy(x_hbm, xs, in_sem.at[0])
    in_t = pltpu.make_async_copy(t_hbm, ts, in_sem.at[1])
    in_x.start()
    in_t.start()

    for k, w in enumerate((wq, wk, wv, wo)):
        W[f, k * 288 : k * 288 + 256, :] = w[...]
        W[f, k * 288 + 256 : k * 288 + 288, 0:64] = wd[k * 32 : k * 32 + 32, :]
        W[f, k * 288 + 256 : k * 288 + 288, 64:128] = wd[128 + k * 32 : 160 + k * 32, :]
    kv[...] = jnp.zeros_like(kv)
    acc[...] = jnp.zeros_like(acc)

    barrier = pltpu.get_barrier_semaphore()
    greet = [sib]
    greet += [dev((x + o) % 4, y, z, c) for o in (1, 2, 3)]
    greet += [dev(x, (y + o) % 8, z, c) for o in range(1, 8)]
    greet += [dev(x, y, (z + o) % 8, c) for o in range(1, 8)]
    other = z + 1 - 2 * zl
    greet += [dev(x, (y + o) % 8, other, c) for o in range(1, 8)]
    for to in greet:
        pl.semaphore_signal(barrier, inc=1, device_id=to)
    pl.semaphore_wait(barrier, len(greet))

    pairs = [h, (h + 3 + 2 * zl) % 4, (h + 1 + 2 * (1 - zl) * 0 + 2 * zl) % 4, (h + 2) % 4]
    pairs[1] = (h + 3 + 2 * zl) % 4
    pairs[2] = (h + 1 + 2 * zl) % 4

    def region(block, core):
        dy, pair, half = block
        rows = (core * 2 + (half + x) % 2) * 288
        return W.at[pairs[pair] * 8 + (y + dy) % 8, pl.ds(pl.multiple_of(rows, 16), 288), :]

    sends, shares, when_in = {}, {}, {}
    for r, row in enumerate(ROUNDS):
        for d, block in enumerate(row):
            if block is not None:
                a = region(block, c)
                sends[r, d] = remote(a, a, ag_s.at[r, d], ag_r.at[r, d], ways[d])
                got = arrives(d, block)
                b = region(got, c)
                shares[r, d] = remote(b, b, cc_s.at[r, d], cc_r.at[r, d], sib)
                when_in[got] = (r, d)

    def norm_rows():
        in_x.wait()
        in_t.wait()
        width = 1024

        def sums(i, carry):
            xx, xt = carry
            cols = pl.ds(pl.multiple_of(i * width, width), width)
            a = xs[:, cols].astype(f32)
            b = ts[:, cols].astype(f32)
            return xx + jnp.sum(a * a, axis=1, keepdims=True), xt + jnp.sum(a * b, axis=1, keepdims=True)

        zero = jnp.zeros((128, 1), f32)
        xx, xt = lax.fori_loop(0, 8192 // width, sums, (zero, zero))
        stat[0] = jnp.broadcast_to(xx, (128, 128))
        stat[1] = jnp.broadcast_to(xt, (128, 128))
        inv = lax.rsqrt(xx / 8192.0 + eps_norm)

        def rows(i, carry):
            cols = pl.ds(pl.multiple_of(i * width, width), width)
            nx[:, cols] = (xs[:, cols].astype(f32) * inv * scale[:, cols]).astype(bf16)
            return carry

        lax.fori_loop(0, 8192 // width, rows, 0)
        lane = lax.broadcasted_iota(jnp.int32, (128, 128), 1)
        token = lax.broadcasted_iota(jnp.int32, (128, 128), 0)
        position = (x * 64 + token % 64).astype(f32)
        rate = jnp.exp((lane % 64).astype(f32) * (-2.0 / 128.0 * math.log(theta_base)))
        angle = position * rate
        stat[2] = jnp.cos(angle)
        sine = jnp.sin(angle)
        stat[3] = jnp.where(lane < 64, -sine, sine)

    def multiply(dy):
        def body(hh, carry):
            g = hh * 8 + (y + dy) % 8
            cols = pl.ds(pl.multiple_of(g * 256, 256), 256)
            a, raw, tgt = nx[:, cols], xs[:, cols], ts[:, cols]
            qk = jnp.concatenate([W[g, 0:256, :], W[g, 288:544, :]], axis=1)
            out = W[g, 864:1120, :]
            down = jnp.concatenate([W[g, 288 * k + 256 : 288 * k + 288, :] for k in range(4)], axis=0)
            both = dot(a, qk)
            acc[0] += both[:, 0:128]
            acc[1] += both[:, 128:256]
            acc[2] += dot(a, W[g, 576:832, :])
            acc[3] += dot(a[:, 0:128], down)
            acc[4] += dot(a[:, 128:256], down)
            acc[5] += dot(raw, out)
            acc[6] += dot(tgt, out)
            acc[7] += dot_general(out, out, 0, 0)
            return carry

        lax.fori_loop(0, 4, body, 0)

    last = {}
    for block, (r, d) in when_in.items():
        last[block[0]] = max(last.get(block[0], 0), r)
    for r in range(len(ROUNDS) + LAG + 1):
        if r >= LAG:
            for d in range(6):
                if (r - LAG, d) in sends:
                    sends[r - LAG, d].wait_recv()
        for d in range(6):
            if (r, d) in sends:
                sends[r, d].start()
        if r >= LAG:
            for d in range(6):
                if (r - LAG, d) in sends:
                    shares[r - LAG, d].start()
        if r == LAG - 1:
            norm_rows()
        for dy in range(8):
            if last[dy] == r - LAG - 1:
                for block, where in when_in.items():
                    if block[0] == dy:
                        shares[where].wait_recv()
                multiply(dy)

    def rope(v):
        return (v * stat[2] + pltpu.roll(v, 64, 1) * stat[3]).astype(bf16)

    q = rope(acc[0])
    own = pl.ds(pl.multiple_of(x * 64, 64), 64)
    d_in = (acc[3][:, 0:64] + acc[4][:, 64:128]).astype(bf16)
    base = acc[2]
    k_own = rope(acc[1])
    v_ref = base.astype(bf16)
    v_pol = (base + dot(d_in, aup[...])).astype(bf16)
    for b in range(2):
        kv[0, b, own, :] = k_own[b * 64 : b * 64 + 64]
        kv[1, b, own, :] = v_ref[b * 64 : b * 64 + 64]
        kv[2, b, own, :] = v_pol[b * 64 : b * 64 + 64]
    kv_own = kv.at[:, :, own, :]
    kvs = [remote(kv_own, kv_own, kv_s.at[o], kv_r.at[o], dev((x + o) % 4, y, z, c)) for o in range(4)]
    for o in (1, 2, 3):
        @pl.when(x + o < 4)
        def _():
            kvs[o].start()

    g_hi = acc[7].astype(bf16)
    g_lo = (acc[7] - g_hi.astype(f32)).astype(bf16)
    for key in sends:
        sends[key].wait_send()
        shares[key].wait_send()
    for o in (1, 2, 3):
        @pl.when(x - o >= 0)
        def _():
            kvs[o].wait_recv()

    row = lax.broadcasted_iota(jnp.int32, (64, 256), 0)
    col = lax.broadcasted_iota(jnp.int32, (64, 256), 1)
    allowed = col <= row + x * 64
    mixed = [[], []]
    for b in range(2):
        s = dot_general(q[b * 64 : b * 64 + 64], kv[0, b], 1, 1) / math.sqrt(128.0)
        s = jnp.where(allowed, s, -1e30)
        e = jnp.exp(s - jnp.max(s, axis=1, keepdims=True))
        e = jnp.where(allowed, e, 0.0)
        w = (e / jnp.sum(e, axis=1, keepdims=True)).astype(bf16)
        att[b] = w
        for m in range(2):
            mixed[m].append(dot(w, kv[1 + m, b]).astype(bf16))

    xx, xt, po, to = stat[0][:, 0:1], stat[1][:, 0:1], acc[5], acc[6]
    logits, invs, projs = [], [], []
    for m in range(2):
        mix = jnp.concatenate(mixed[m], axis=0)
        mg = dot(mix, g_hi) + dot(mix, g_lo)
        mixf = mix.astype(f32)
        sq = xx + jnp.sum(mixf * (2.0 * po + mg), axis=1, keepdims=True)
        inv = lax.rsqrt(sq / 8192.0 + eps_norm)
        logits.append(inv * (xt + jnp.sum(mixf * to, axis=1, keepdims=True)))
        invs.append(inv)
        projs.append(po + mg)
    token = lax.broadcasted_iota(jnp.int32, (128, 1), 0)
    start = jnp.where(token < 64, 256 - rlen[0], 256 - rlen[1])
    sign = jnp.where(token < 64, 1.0, -1.0)
    resp = jnp.where(x * 64 + token % 64 >= start, sign, 0.0)
    part = jnp.sum(resp * (logits[1] - logits[0]), axis=0, keepdims=True)
    mgs[...] = jnp.broadcast_to(part, (8, 128))
    mgc = [remote(mgs, mgr.at[o], mg_s.at[o], mg_r.at[o], dev((x + o) % 4, y, z, c)) for o in range(4)]
    for o in (1, 2, 3):
        mgc[o].start()

    head = (resp * invs[1] * (to - (logits[1] / 8192.0) * invs[1] * projs[1])).astype(bf16)
    for b in range(2):
        terms = dot_general(att[b], head[b * 64 : b * 64 + 64], 0, 0)
        vgs[b] = terms.astype(bf16)
        vgo[b] = terms
    vgc = []
    for o in range(4):
        target = (x + 4 - o) % 4
        src = vgs.at[:, pl.ds(pl.multiple_of(target * 64, 64), 64), :]
        vgc.append(remote(src, vgr.at[o], vg_s.at[o], vg_r.at[o], dev(target, y, z, c)))
    for o in (1, 2, 3):
        @pl.when(x - o >= 0)
        def _():
            vgc[o].start()
    for o in (1, 2, 3):
        mgc[o].wait()
    margin = beta_dpo * (mgs[...] + mgr[1] + mgr[2] + mgr[3])
    pull = (-beta_dpo / 128.0) / (1.0 + jnp.exp(margin))
    loss = jnp.maximum(-margin, 0.0) + jnp.log1p(jnp.exp(-jnp.abs(margin)))
    mine = [vgo[b, own, :] for b in range(2)]
    total = jnp.concatenate(mine, axis=0)
    vgo[0, 0:128, :] = total
    for o in (1, 2, 3):
        @pl.when(x + o < 4)
        def _():
            vgc[o].wait_recv()
            vgo[0, 0:128, :] += vgr[o].reshape(128, 128).astype(f32)
    vg = (vgo[0, 0:128, :] * pull[0:1, :]).astype(bf16)

    up = dot_general(d_in, vg, 0, 0)
    agt = dot_general(aup[...], vg, 1, 1).astype(bf16)

    us[...] = up
    keep = pl.ds(pl.multiple_of(c * 32, 32), 32)
    give = pl.ds(pl.multiple_of(32 - c * 32, 32), 32)
    ucs[32:40, :] = loss
    ucs[0:32, :] = us[give, :]
    uc = remote(ucs, ucr, uc_s.at[0], uc_r.at[0], sib)
    uc.start()

    ag_keep = jnp.where(c == 0, agt[0:32], agt[32:64])
    ag_give = jnp.where(c == 0, agt[32:64], agt[0:32])
    dcs = []
    for n in range(4):
        def give_body(i, carry):
            g = n * 8 + i
            cols = pl.ds(pl.multiple_of(g * 256, 256), 256)
            dsend[g] = dot(ag_give, nx[:, cols]).astype(bf16)
            return carry
        lax.fori_loop(0, 8, give_body, 0)
        cp = remote(dsend.at[pl.ds(n * 8, 8)], drecv.at[pl.ds(n * 8, 8)], dc_s.at[n], dc_r.at[n], sib)
        cp.start()
        dcs.append(cp)

    def keep_body(g, carry):
        cols = pl.ds(pl.multiple_of(g * 256, 256), 256)
        dkeep[g] = dot(ag_keep, nx[:, cols])
        return carry
    lax.fori_loop(0, 32, keep_body, 0)

    uc.wait()
    uxs[0:32, :] = us[keep, :] + ucr[0:32, :]
    uxs[32:40, :] = loss + ucr[32:40, :]
    uxc = [remote(uxs, uxr.at[o], ux_s.at[o], ux_r.at[o], dev((x + o) % 4, y, z, c)) for o in range(4)]
    for o in (1, 2, 3):
        uxc[o].start()

    for n in range(4):
        dcs[n].wait_recv()
        def add_body(i, carry):
            g = n * 8 + i
            s1[n, i] = (dkeep[g] + drecv[g].astype(f32)).astype(bf16)
            return carry
        lax.fori_loop(0, 8, add_body, 0)

    y1, z1 = [], []
    for o in range(8):
        ty, tz = (y + o) % 8, (z + o) % 8
        y1.append(remote(s1.at[:, ty, pl.ds(0, 16), :], r1y.at[o], y1_s.at[o], y1_r.at[o], dev(x, ty, z, c)))
        z1.append(remote(s1.at[tz // 2, pl.ds((tz % 2) * 4, 4), pl.ds(16, 16), :], r1z.at[o], z1_s.at[o], z1_r.at[o],
                         dev(x, y, tz, c)))
    for o in (4, 3, 5, 2, 6, 1, 7):
        y1[o].start()
        z1[o].start()
    for o in (1, 2, 3):
        uxc[o].wait()
    uys[...] = uxs[...] + uxr[1] + uxr[2] + uxr[3]
    uyc = [remote(uys, uyr.at[o], uy_s.at[o], uy_r.at[o], dev(x, (y + o) % 8, z, c)) for o in range(8)]
    for o in range(1, 8):
        uyc[o].start()
    for o in range(1, 8):
        y1[o].wait()
        z1[o].wait()
    sy = s1[:, y, 0:16, :].astype(f32)
    sz = s1[h, pl.ds(zl * 4, 4), 16:32, :].astype(f32)
    for o in range(1, 8):
        sy += r1y[o].astype(f32)
        sz += r1z[o].astype(f32)
    s2y[...] = sy.astype(bf16)
    s2z[...] = sz.astype(bf16)

    y2 = []
    for o in range(8):
        tz = (z + o) % 8
        y2.append(remote(s2y.at[tz // 2], r2y.at[o], y2_s.at[o], y2_r.at[o], dev(x, y, tz, c)))
    for o in range(1, 8):
        y2[o].start()
    z2 = []
    for j in range(4):
        for zz in range(2):
            ty = zl * 4 + j
            z2.append((remote(s2z.at[j], r2z.at[y], z2_s.at[j * 2 + zz], z2_r.at[y], dev(x, ty, h * 2 + zz, c)),
                       jnp.logical_and(ty == y, zz == zl), j))
    for cp, me, j in z2:
        @pl.when(jnp.logical_not(me))
        def _():
            cp.start()
        @pl.when(me)
        def _():
            r2z[y] = s2z[j]
    for o in range(1, 8):
        uyc[o].wait()
    tot = uys[...]
    for o in range(1, 8):
        tot += uyr[o]
    uzs[...] = tot
    uzc = [remote(uzs, uzr.at[o], uz_s.at[o], uz_r.at[o], dev(x, y, (z + o) % 8, c)) for o in range(8)]
    for o in range(1, 8):
        uzc[o].start()
    for o in range(1, 8):
        y2[o].wait()
    for cp, me, j in z2:
        @pl.when(jnp.logical_not(me))
        def _():
            cp.wait_send()
    for s in range(8):
        @pl.when(jnp.logical_not(jnp.logical_and(s == y, y // 4 == zl)))
        def _():
            remote(s2z.at[0], r2z.at[s], z2_s.at[0], z2_r.at[s], sib).wait_recv()
    ty_ = s2y[h].astype(f32)
    tz_ = r2z[0].astype(f32)
    for o in range(1, 8):
        ty_ += r2y[o].astype(f32)
        tz_ += r2z[o].astype(f32)
    for k in range(2):
        s3[k, 0:16, :] = ty_[:, k * 128 : k * 128 + 128]
        s3[k, 16:32, :] = tz_[:, k * 128 : k * 128 + 128]

    x3 = []
    for o in range(4):
        tx = (x + o) % 4
        x3.append(remote(s3.at[tx // 2], r3.at[o], x3_s.at[o], x3_r.at[o], dev(tx, y, z, c)))
    for o in (1, 2, 3):
        x3[o].start()
    for o in range(1, 8):
        uzc[o].wait()
    tot = uzs[...]
    for o in range(1, 8):
        tot += uzr[o]
    ues[...] = tot[0:32, :]
    ue = remote(ues, uer, ue_s.at[0], ue_r.at[0], sib)
    ue.start()
    loss_ref[...] = tot[32:40, :] * (1.0 / 512.0)
    for o in (1, 2, 3):
        x3[o].wait()
    mine = s3[x // 2] + r3[1] + r3[2] + r3[3]
    s4[...] = mine
    c4 = remote(s4, r4, c4_s.at[0], c4_r.at[0], sib)
    c4.start()
    ue.wait()
    gup_ref[keep, :] = ues[...]
    gup_ref[give, :] = uer[...]
    for o in (1, 2, 3):
        @pl.when(x + o < 4)
        def _():
            kvs[o].wait_send()
        @pl.when(x - o >= 0)
        def _():
            vgc[o].wait_send()
    for n in range(4):
        dcs[n].wait_send()
    c4.wait()
    low = jnp.where(c == 0, s4[...], r4[...])
    high = jnp.where(c == 0, r4[...], s4[...])
    whole = jnp.concatenate([low, high], axis=0)
    whole = jnp.where(x % 2 == 0, whole, pltpu.roll(whole, 64, 1))
    gdown_ref[...] = whole.T[0:64, :]


def step(x_in, t_in, rlen, scale, wq, wk, wv, wo, wd, aup):
    f32, bf16 = jnp.float32, jnp.bfloat16
    V = pltpu.VMEM
    D = pltpu.SemaphoreType.DMA
    n = len(ROUNDS)
    vm = pl.BlockSpec(memory_space=pltpu.VMEM)
    hb = pl.BlockSpec(memory_space=pl.ANY)
    loss, gdown, gup = pl.pallas_call(
        kernel,
        name="dpo_step",
        out_shape=(
            jax.ShapeDtypeStruct((8, 128), f32),
            jax.ShapeDtypeStruct((64, 64), f32),
            jax.ShapeDtypeStruct((64, 128), f32),
        ),
        in_specs=[hb, hb, pl.BlockSpec(memory_space=pltpu.SMEM)] + [vm] * 7,
        out_specs=(vm, vm, vm),
        scratch_shapes=[
            V((128, 8192), bf16), V((128, 8192), bf16), V((128, 8192), bf16),
            V((32, 1152, 128), bf16), V((8, 128, 128), f32), V((3, 2, 256, 128), bf16), V((2, 64, 256), bf16),
            V((2, 256, 128), bf16), V((4, 2, 64, 128), bf16), V((2, 256, 128), f32), V((8, 128), f32), V((4, 8, 128), f32),
            V((32, 32, 256), f32), V((32, 32, 256), bf16), V((32, 32, 256), bf16), V((4, 8, 32, 256), bf16),
            V((8, 4, 16, 256), bf16), V((8, 4, 16, 256), bf16), V((4, 16, 256), bf16), V((4, 16, 256), bf16),
            V((8, 16, 256), bf16), V((8, 16, 256), bf16), V((2, 32, 128), f32), V((4, 32, 128), f32),
            V((32, 128), f32), V((32, 128), f32),
            V((64, 128), f32), V((64, 128), f32), V((40, 128), f32), V((4, 40, 128), f32), V((40, 128), f32),
            V((8, 40, 128), f32), V((40, 128), f32), V((8, 40, 128), f32), V((40, 128), f32), V((40, 128), f32), V((32, 128), f32), V((32, 128), f32),
            V((4, 128, 128), f32),
            D((2,)), D((n, 6)), D((n, 6)), D((n, 6)), D((n, 6)), D((4,)), D((4,)), D((4,)), D((4,)), D((4,)), D((4,)),
            D((4,)), D((4,)), D((8,)), D((8,)), D((8,)), D((8,)), D((8,)), D((8,)), D((8,)), D((8,)), D((4,)), D((4,)),
            D((1,)), D((1,)), D((1,)), D((1,)), D((4,)), D((4,)), D((8,)), D((8,)), D((8,)), D((8,)), D((1,)), D((1,)),
        ],
        compiler_params=pltpu.CompilerParams(
            collective_id=0, has_side_effects=True, vmem_limit_bytes=56 * 2**20
        ),
    )(
        x_in.reshape(128, 8192), t_in.reshape(128, 8192), rlen, scale.reshape(1, 8192), wq, wk, wv, wo, wd, aup
    )
    return loss[0, 0], gdown, gup


def solution(mesh):
    return jax.shard_map(
        step,
        mesh=mesh,
        in_specs=(
            P(("dp", "fsdp"), "seq", None),
            P(("dp", "fsdp"), "seq", None),
            P(("dp", "fsdp")),
            P(),
            P("fsdp", None),
            P("fsdp", None),
            P("fsdp", None),
            P("fsdp", None),
            P("fsdp", None),
            P(),
        ),
        out_specs=(P(), P(("fsdp", "seq"), None), P()),
        check_vma=False,
    )
```

time: 1280 us -> 104 us (0.08)
  waiting for transfers between devices: 653 us -> 0 us
  blocking collectives: 566 us -> 0 us
  Pallas kernels: 0 us -> 98 us
  matrix products: 22.7 us -> 0 us
  other arithmetic: 21.4 us -> 0 us
  between operations: 17.6 us -> 0.64 us
    psum x4 -> x0, blocking collectives: 537 us -> none  [the longest x1 291 us: on_device(): dpo_loss = lax.psum(jax.nn.softplus(-margin), ('dp', 'fsdp')) / pair_count]
    all_gather x5 -> x0, waiting for transfers between devices: 378 us -> none  [the longest x1 83.9 us: on_device(): lax.all_gather(key_weight, 'fsdp', axis=0, tiled=True)]
    reduce_scatter x2 -> x0, waiting for transfers between devices: 272 us -> none  [the longest x1 250 us: on_device(): lax.psum_scatter(down_product, ('fsdp', 'seq'), scatter_dimension=0, tile...]
    pallas_call x0 -> x1, Pallas kernels: none -> 98 us  [step(): pl.pallas_call(kernel, name='dpo_step', out_shape=(jax.ShapeDtypeStruct((...]
    all_gather x3 -> x0, blocking collectives: 29.6 us -> none  [the longest x1 9.92 us: on_device(): lax.all_gather(value_ref, 'seq', axis=1, tiled=True)]
    dot_general x12 -> x0, matrix products: 22.7 us -> none  [the longest x4 10.4 us: on_device(): jnp.dot(columns, weight_rows, preferred_element_type=jnp.float32)]
  transfers between devices with their start and end apart: 7 -> 0, of which waited for: 7 -> 0; matrix products, arithmetic and copies ran while one was open for 2% -> 0% of each run, Pallas kernels for 0% -> 0%
where the time goes in v1:
time: 104 us
  Pallas kernels  98 us (94%)
  local copies, waits for them, and re-layouts  5.42 us (5%)
    pallas_call x1, Pallas kernels, step(): pl.pallas_call(kernel, name='dpo_step', out_shape=(jax.ShapeDtypeStruct((...  98 us
    unnamed x3, local copies, waits for them, and re-layouts  4.23 us

profile of v1, /device:TPU:1, one launch (start us, length us, event | category | flops | bytes accessed | tf_op | source)
XLA Modules:
  0.0 104.1 jit_solution(3168943785020929796)
XLA Ops:
  0.6 1.5 %copy.13.wd = bf16[256,64]{1,0:T(8,128)(2,1)} copy(bf16[256,64]{0,1:T(8,128)(2,1)} %param.18) | data formatting | bytes 65536 | tf_op args[8]
  2.1 98.0 %dpo_step.1 = (f32[8,128]{1,0:T(8,128)}, f32[64,64]{1,0:T(8,128)}, f32[64,128]{1,0:T(8,128)}) custom-call(bf16[128,8192]{1,0:T(8,128)(2,1)} %bitcast.4, bf16[128,8192]{1,0:T(8,128)(2,1)} %bitcast.5, s32[2]{0:T(128)} %rlen.1, f32[1,8192]{1,0:T(1,128)} %bitcast.6, bf16[256,128]{1,0:T(8,128)(2,1)} %wq.1, bf16[256,128]{1,0:T(8,128)(2,1)} %wk.1, ...), custom_call_target="tpu_custom_call" | custom-call | tf_op jit(solution)/shard_map/dpo_step/pallas_call | solution.py:455
  100.1 1.2 %slice.3 = f32[1,1]{1,0:T(1,128)} slice(f32[8,128]{1,0:T(8,128)} %get-tuple-element.6), slice={[0:1], [0:1]} | slice | bytes 8 | tf_op jit(solution)/shard_map/slice | solution.py:486
  101.3 1.4 %copy.16 = f32[64,64]{1,0:T(8,128)} copy(f32[64,64]{1,0:T(8,128)} %get-tuple-element.13) | data formatting | bytes 32768
  102.7 1.4 %copy.17 = f32[64,128]{1,0:T(8,128)} copy(f32[64,128]{1,0:T(8,128)} %get-tuple-element.14) | data formatting | bytes 65536

commit v2 on v1

--- a/solution.py
+++ b/solution.py
@@ -11,34 +11,60 @@
 beta_dpo = 0.1
 eps_norm = 1e-05
 
-LAG = 2
-ROUNDS = [[None, None, (0, 0, 0), (0, 0, 1), (0, 0, 0), None], [None, None, (0, 0, 1), (0, 0, 0), (0, 0, 1), None], [None, None, (7, 0, 0), (1, 0, 1), (1, 0, 1), (0, 1, 0)], [None, None, (7, 0, 1), (1, 0, 0), (7, 0, 1), (0, 1, 1)], [None, (1, 1, 1), (6, 0, 0), (2, 0, 1), (0, 2, 0), (1, 1, 1)], [None, (7, 1, 1), (6, 0, 1), (2, 0, 0), (0, 2, 1), (7, 1, 1)], [(1, 2, 1), None, (0, 3, 0), (1, 2, 1), (3, 0, 1), None], [(7, 2, 1), None, (7, 2, 1), (0, 3, 0), (5, 0, 1), None], [(2, 2, 1), (3, 1, 1), (7, 3, 0), (3, 1, 1), (2, 2, 1), (3, 1, 1)], [(5, 1, 1), (6, 2, 1), (5, 0, 1), (1, 3, 0), (6, 2, 1), (5, 1, 1)], [(4, 1, 1), (3, 2, 1), (6, 3, 0), (3, 0, 0), (3, 2, 1), (4, 1, 1)], [(7, 3, 0), (5, 2, 1), (7, 1, 0), (2, 3, 0), (5, 2, 1), (2, 2, 1)], [(4, 2, 1), (1, 3, 0), (5, 3, 0), (1, 1, 0), (4, 2, 1), (6, 2, 1)]]
-
-
-def arrives(way, block):
-    dy, pair, half = block
+PARTS = 2
+SENDS = 124
+GATHER = (
+    (0,4,0,0,1,0), (0,3,0,0,0,0), (0,2,0,0,1,1), (0,2,0,0,0,0), (0,3,0,0,0,1), (0,4,0,0,0,1), (0,3,0,0,1,0),
+    (0,4,0,0,1,1), (0,2,0,0,0,1), (2,), (0,3,0,0,1,1), (0,2,0,0,1,0), (0,4,0,0,0,0), (1,0), (0,5,0,1,1,0), (1,2),
+    (0,2,7,0,1,1), (1,1), (0,3,1,0,0,0), (0,4,1,0,0,0), (1,5), (0,5,0,1,0,1), (1,4), (0,3,1,0,0,1), (0,4,7,0,1,1),
+    (1,3), (0,2,7,0,0,0), (1,7), (0,5,0,1,1,1), (0,2,0,1,1,0), (0,4,1,0,0,1), (1,6), (0,3,1,0,1,0), (1,11),
+    (0,5,0,1,0,0), (1,9), (0,3,1,0,1,1), (1,10), (0,2,7,0,1,0), (1,8), (0,4,7,0,0,1), (1,15), (0,5,1,1,0,0), (1,13),
+    (0,0,6,0,1,1), (0,1,1,1,0,0), (0,2,6,0,1,1), (1,14), (0,3,2,0,0,0), (1,12), (0,4,0,2,1,0), (1,18), (0,5,7,1,1,1),
+    (1,19), (0,2,6,0,0,0), (1,17), (0,3,2,0,0,1), (1,16), (0,4,0,2,0,1), (1,21), (0,5,7,1,1,0), (1,22),
+    (0,1,1,1,0,1), (0,0,7,1,1,0), (0,2,7,1,1,0), (1,23), (0,4,2,0,1,0), (1,20), (0,3,0,2,1,1), (1,27), (0,5,7,1,0,1),
+    (3,0,1,4,28), (0,2,7,1,0,1), (0,3,1,1,0,1), (0,4,0,2,1,1), (1,28), (0,0,1,2,0,0), (0,5,1,1,0,1), (1,33),
+    (0,1,0,3,1,0), (0,2,0,3,1,0), (0,3,1,2,0,0), (0,4,1,2,0,0), (1,24), (1,25), (1,26), (1,31), (0,0,5,0,1,1),
+    (1,36), (0,1,3,0,0,1), (1,37), (0,3,0,3,0,1), (1,34), (0,2,7,2,1,1), (0,4,7,2,1,1), (1,29), (1,30), (1,32),
+    (1,40), (0,5,7,1,0,0), (1,35), (0,0,5,0,0,0), (0,1,3,0,0,0), (1,41), (0,2,6,1,1,0), (1,43), (0,3,1,2,1,1),
+    (0,4,3,0,0,0), (0,5,6,1,1,0), (0,0,6,1,1,0), (1,46), (0,1,2,1,0,1), (0,2,5,0,1,1), (0,4,5,0,1,1), (0,3,0,3,1,0),
+    (1,38), (1,39), (1,42), (1,45), (0,0,6,1,0,1), (0,5,6,1,0,1), (1,51), (0,1,7,3,1,0), (0,2,7,3,1,0),
+    (0,4,3,0,0,1), (1,52), (0,3,2,2,0,0), (1,44), (1,47), (0,0,2,2,0,0), (0,5,2,1,0,1), (1,56), (0,1,1,3,0,1),
+    (0,3,1,3,0,1), (1,58), (0,2,7,3,1,1), (0,4,2,2,0,0), (1,48), (1,49), (1,50), (1,53), (0,5,2,2,0,0),
+    (3,2,8,24,29), (0,0,7,3,1,1), (1,62), (0,1,5,1,1,0), (1,55), (0,4,3,0,1,1), (1,63), (0,3,2,2,1,1), (0,2,5,1,1,0),
+    (1,54), (1,57), (1,65), (0,0,6,2,1,0), (0,5,5,1,1,0), (1,68), (0,1,4,0,1,1), (0,4,2,2,1,1), (0,2,6,2,1,1),
+    (0,3,3,0,0,0), (1,59), (1,60), (1,61), (1,64), (1,69), (0,0,5,1,1,1), (1,75), (0,5,3,1,0,1), (1,76),
+    (0,1,3,2,0,0), (0,4,3,2,0,0), (1,74), (0,2,6,3,1,0), (0,3,3,2,0,0), (1,66), (1,67), (1,70), (0,0,6,3,1,0),
+    (1,81), (0,1,6,3,1,1), (0,4,4,0,1,1), (0,2,6,3,1,1), (1,80), (0,3,2,3,0,1), (1,71), (1,72), (1,73), (1,85),
+    (0,5,5,1,0,0), (1,82), (0,0,2,3,0,0), (1,88), (0,1,4,1,1,0), (1,87), (0,4,3,2,1,1), (0,2,6,2,0,1), (0,3,3,2,1,1),
+    (1,77), (1,78), (1,79), (0,5,4,1,1,0), (0,0,3,1,0,0), (1,94), (0,1,4,0,0,0), (1,91), (0,4,4,0,0,1), (1,83),
+    (1,84), (1,86), (1,96), (0,3,3,2,0,1), (3,3,5,6,12,20,30), (1,99), (0,2,5,3,1,0), (0,0,5,3,1,0), (1,98),
+    (0,1,3,3,0,0), (1,100), (0,4,4,2,0,0), (1,89), (1,90), (1,92), (1,93), (1,105), (0,3,3,3,0,1), (1,104),
+    (0,0,5,3,1,1), (0,2,5,3,1,1), (1,95), (1,97), (1,101), (1,102), (1,103), (1,106), (1,107), (1,108), (1,109),
+    (1,110), (1,111), (1,112), (1,113), (1,114), (1,115), (1,116), (1,117), (1,118), (1,119), (1,120), (1,121),
+    (1,122), (1,123), (3,7,9,10,11,13,14,15,16,17,18,19,21,22,23,25,26,27,31),
+)
+
+def arrives(way, piece):
+    dy, pair, half, part = piece
     if way < 2:
-        return (dy, pair, 1 - half)
+        return (dy, pair, 1 - half, part)
     if way == 2:
-        return ((dy - 1) % 8, pair, half)
+        return ((dy - 1) % 8, pair, half, part)
     if way == 3:
-        return ((dy + 1) % 8, pair, half)
+        return ((dy + 1) % 8, pair, half, part)
     if way == 4:
-        return (dy, (1, 0, 3, 2)[pair], half)
-    return (dy, (0, 2, 1, 3)[pair], half)
-
+        return (dy, (1, 0, 3, 2)[pair], half, part)
+    return (dy, (0, 2, 1, 3)[pair], half, part)
 
 def dot(a, b):
     return jnp.dot(a, b, preferred_element_type=jnp.float32)
 
-
 def dot_general(a, b, ca, cb):
     return lax.dot_general(a, b, (((ca,), (cb,)), ((), ())), preferred_element_type=jnp.float32)
 
-
 def kernel(
     x_hbm, t_hbm, rlen, scale, wq, wk, wv, wo, wd, aup,
-    loss_ref, gdown_ref, gup_ref,
+    out_ref,
     xs, ts, nx, W, acc, kv, att, vgs, vgr, vgo, mgs, mgr,
     dkeep, dsend, drecv, s1, r1y, r1z, s2y, s2z, r2y, r2z, s3, r3, s4, r4,
     us, ur, uxs, uxr, uys, uyr, uzs, uzr, ucs, ucr, ues, uer, stat,
@@ -76,8 +102,7 @@
 
     for k, w in enumerate((wq, wk, wv, wo)):
         W[f, k * 288 : k * 288 + 256, :] = w[...]
-        W[f, k * 288 + 256 : k * 288 + 288, 0:64] = wd[k * 32 : k * 32 + 32, :]
-        W[f, k * 288 + 256 : k * 288 + 288, 64:128] = wd[128 + k * 32 : 160 + k * 32, :]
+        W[f, k * 288 + 256 : k * 288 + 288, :] = wd[(k % 2) * 32 : (k % 2) * 32 + 32, (k // 2) * 128 : (k // 2) * 128 + 128]
     kv[...] = jnp.zeros_like(kv)
     acc[...] = jnp.zeros_like(acc)
 
@@ -96,21 +121,38 @@
     pairs[1] = (h + 3 + 2 * zl) % 4
     pairs[2] = (h + 1 + 2 * zl) % 4
 
-    def region(block, core):
-        dy, pair, half = block
-        rows = (core * 2 + (half + x) % 2) * 288
+    def region(piece):
+        dy, pair, half, part = piece
+        rows = (c * 2 + (half + x) % 2) * 288 + part * (288 // PARTS)
+        return W.at[pairs[pair] * 8 + (y + dy) % 8, pl.ds(pl.multiple_of(rows, 16), 288 // PARTS), :]
+
+    groups = [do[1:] for do in GATHER if do[0] == 3]
+    group_of = {block: k for k, blocks in enumerate(groups) for block in blocks}
+    sends, came = [], []
+    for do in GATHER:
+        if do[0] == 0:
+            n = len(sends)
+            a = region(do[2:])
+            came.append(arrives(do[1], do[2:]))
+            sends.append(remote(a, a, ag_s.at[0], ag_r.at[n], ways[do[1]]))
+
+    def half_block(dy, pair, half):
+        rows = (c * 2 + (half + x) % 2) * 288
         return W.at[pairs[pair] * 8 + (y + dy) % 8, pl.ds(pl.multiple_of(rows, 16), 288), :]
 
-    sends, shares, when_in = {}, {}, {}
-    for r, row in enumerate(ROUNDS):
-        for d, block in enumerate(row):
-            if block is not None:
-                a = region(block, c)
-                sends[r, d] = remote(a, a, ag_s.at[r, d], ag_r.at[r, d], ways[d])
-                got = arrives(d, block)
-                b = region(got, c)
-                shares[r, d] = remote(b, b, cc_s.at[r, d], cc_r.at[r, d], sib)
-                when_in[got] = (r, d)
+    def whole(blocks, sem):
+        ref = W.at[pl.ds(0, blocks), pl.ds(0, 576), :]
+        return pltpu.make_async_copy(ref, ref, sem)
+
+    parts_in = {}
+
+    def arrive(n):
+        dy, pair, half, _ = came[n]
+        sends[n].wait_recv()
+        parts_in[dy, pair, half] = parts_in.get((dy, pair, half), 0) + 1
+        if parts_in[dy, pair, half] == PARTS:
+            a = half_block(dy, pair, half)
+            remote(a, a, cc_s.at[0], cc_r.at[group_of[dy * 4 + pair]], sib).start()
 
     def norm_rows():
         in_x.wait()
@@ -145,57 +187,51 @@
         sine = jnp.sin(angle)
         stat[3] = jnp.where(lane < 64, -sine, sine)
 
-    def multiply(dy):
-        def body(hh, carry):
-            g = hh * 8 + (y + dy) % 8
+    def multiply(blocks):
+        whole(len(blocks) - (0 in blocks), cc_r.at[group_of[blocks[0]]]).wait()
+
+        def body(i, carry):
+            g = jnp.int32(0)
+            for k, block in enumerate(blocks):
+                g += jnp.where(i == k, 1, 0) * (pairs[block % 4] * 8 + (y + block // 4) % 8)
             cols = pl.ds(pl.multiple_of(g * 256, 256), 256)
             a, raw, tgt = nx[:, cols], xs[:, cols], ts[:, cols]
             qk = jnp.concatenate([W[g, 0:256, :], W[g, 288:544, :]], axis=1)
             out = W[g, 864:1120, :]
-            down = jnp.concatenate([W[g, 288 * k + 256 : 288 * k + 288, :] for k in range(4)], axis=0)
+            down = jnp.concatenate(
+                [jnp.concatenate([W[g, 288 * k + 256 : 288 * k + 288, :] for k in (k0, k0 + 1)], axis=0) for k0 in (0, 2)],
+                axis=1,
+            )
             both = dot(a, qk)
             acc[0] += both[:, 0:128]
             acc[1] += both[:, 128:256]
             acc[2] += dot(a, W[g, 576:832, :])
-            acc[3] += dot(a[:, 0:128], down)
-            acc[4] += dot(a[:, 128:256], down)
+            acc[3, :, 0:64] += dot_general(a, down, 1, 1)
             acc[5] += dot(raw, out)
             acc[6] += dot(tgt, out)
             acc[7] += dot_general(out, out, 0, 0)
             return carry
 
-        lax.fori_loop(0, 4, body, 0)
-
-    last = {}
-    for block, (r, d) in when_in.items():
-        last[block[0]] = max(last.get(block[0], 0), r)
-    for r in range(len(ROUNDS) + LAG + 1):
-        if r >= LAG:
-            for d in range(6):
-                if (r - LAG, d) in sends:
-                    sends[r - LAG, d].wait_recv()
-        for d in range(6):
-            if (r, d) in sends:
-                sends[r, d].start()
-        if r >= LAG:
-            for d in range(6):
-                if (r - LAG, d) in sends:
-                    shares[r - LAG, d].start()
-        if r == LAG - 1:
+        lax.fori_loop(0, len(blocks), body, 0, unroll=2)
+
+    n = 0
+    for do in GATHER:
+        if do[0] == 0:
+            sends[n].start()
+            n += 1
+        elif do[0] == 1:
+            arrive(do[1])
+        elif do[0] == 2:
             norm_rows()
-        for dy in range(8):
-            if last[dy] == r - LAG - 1:
-                for block, where in when_in.items():
-                    if block[0] == dy:
-                        shares[where].wait_recv()
-                multiply(dy)
+        else:
+            multiply(do[1:])
 
     def rope(v):
         return (v * stat[2] + pltpu.roll(v, 64, 1) * stat[3]).astype(bf16)
 
     q = rope(acc[0])
     own = pl.ds(pl.multiple_of(x * 64, 64), 64)
-    d_in = (acc[3][:, 0:64] + acc[4][:, 64:128]).astype(bf16)
+    d_in = acc[3, :, 0:64].astype(bf16)
     base = acc[2]
     k_own = rope(acc[1])
     v_ref = base.astype(bf16)
@@ -211,11 +247,22 @@
         def _():
             kvs[o].start()
 
+    def waitkv():
+        for o in (1, 2, 3):
+            @pl.when(x + o < 4)
+            def _():
+                kvs[o].wait_send()
+
+    def waitvg():
+        for o in (1, 2, 3):
+            @pl.when(x - o >= 0)
+            def _():
+                vgc[o].wait_send()
+
     g_hi = acc[7].astype(bf16)
     g_lo = (acc[7] - g_hi.astype(f32)).astype(bf16)
-    for key in sends:
-        sends[key].wait_send()
-        shares[key].wait_send()
+    whole(31, ag_s.at[0]).wait()
+    whole(31, cc_s.at[0]).wait()
     for o in (1, 2, 3):
         @pl.when(x - o >= 0)
         def _():
@@ -251,6 +298,7 @@
     sign = jnp.where(token < 64, 1.0, -1.0)
     resp = jnp.where(x * 64 + token % 64 >= start, sign, 0.0)
     part = jnp.sum(resp * (logits[1] - logits[0]), axis=0, keepdims=True)
+
     mgs[...] = jnp.broadcast_to(part, (8, 128))
     mgc = [remote(mgs, mgr.at[o], mg_s.at[o], mg_r.at[o], dev((x + o) % 4, y, z, c)) for o in range(4)]
     for o in (1, 2, 3):
@@ -296,25 +344,18 @@
     uc = remote(ucs, ucr, uc_s.at[0], uc_r.at[0], sib)
     uc.start()
 
-    ag_keep = jnp.where(c == 0, agt[0:32], agt[32:64])
-    ag_give = jnp.where(c == 0, agt[32:64], agt[0:32])
+    ag_both = jnp.where(c == 0, jnp.concatenate([agt[32:64], agt[0:32]], axis=0), agt)
     dcs = []
     for n in range(4):
-        def give_body(i, carry):
-            g = n * 8 + i
-            cols = pl.ds(pl.multiple_of(g * 256, 256), 256)
-            dsend[g] = dot(ag_give, nx[:, cols]).astype(bf16)
-            return carry
-        lax.fori_loop(0, 8, give_body, 0)
+        for i in range(2):
+            g = n * 8 + i * 4
+            both = dot(ag_both, nx[:, g * 256 : g * 256 + 1024])
+            for k in range(4):
+                dsend[g + k] = both[0:32, k * 256 : k * 256 + 256].astype(bf16)
+                dkeep[g + k] = both[32:64, k * 256 : k * 256 + 256]
         cp = remote(dsend.at[pl.ds(n * 8, 8)], drecv.at[pl.ds(n * 8, 8)], dc_s.at[n], dc_r.at[n], sib)
         cp.start()
         dcs.append(cp)
-
-    def keep_body(g, carry):
-        cols = pl.ds(pl.multiple_of(g * 256, 256), 256)
-        dkeep[g] = dot(ag_keep, nx[:, cols])
-        return carry
-    lax.fori_loop(0, 32, keep_body, 0)
 
     uc.wait()
     uxs[0:32, :] = us[keep, :] + ucr[0:32, :]
@@ -325,11 +366,7 @@
 
     for n in range(4):
         dcs[n].wait_recv()
-        def add_body(i, carry):
-            g = n * 8 + i
-            s1[n, i] = (dkeep[g] + drecv[g].astype(f32)).astype(bf16)
-            return carry
-        lax.fori_loop(0, 8, add_body, 0)
+        s1[n] = (dkeep[n * 8 : n * 8 + 8] + drecv[n * 8 : n * 8 + 8].astype(f32)).astype(bf16)
 
     y1, z1 = [], []
     for o in range(8):
@@ -418,7 +455,7 @@
     ues[...] = tot[0:32, :]
     ue = remote(ues, uer, ue_s.at[0], ue_r.at[0], sib)
     ue.start()
-    loss_ref[...] = tot[32:40, :] * (1.0 / 512.0)
+    out_ref[128:136, :] = tot[32:40, :] * (1.0 / 512.0)
     for o in (1, 2, 3):
         x3[o].wait()
     mine = s3[x // 2] + r3[1] + r3[2] + r3[3]
@@ -426,8 +463,8 @@
     c4 = remote(s4, r4, c4_s.at[0], c4_r.at[0], sib)
     c4.start()
     ue.wait()
-    gup_ref[keep, :] = ues[...]
-    gup_ref[give, :] = uer[...]
+    out_ref[keep, :] = ues[...]
+    out_ref[give, :] = uer[...]
     for o in (1, 2, 3):
         @pl.when(x + o < 4)
         def _():
@@ -442,26 +479,26 @@
     high = jnp.where(c == 0, r4[...], s4[...])
     whole = jnp.concatenate([low, high], axis=0)
     whole = jnp.where(x % 2 == 0, whole, pltpu.roll(whole, 64, 1))
-    gdown_ref[...] = whole.T[0:64, :]
-
+    out_ref[64:128, 0:64] = whole.T[0:64, :]
+    out_ref[64:128, 64:128] = jnp.zeros((64, 64), f32)
+
+def split(packed, loss_ref, gdown_ref, gup_ref):
+    loss_ref[0, 0] = jnp.max(packed[128:136, :])
+    gdown_ref[...] = packed[64:128, 0:64]
+    gup_ref[...] = packed[0:64, :]
 
 def step(x_in, t_in, rlen, scale, wq, wk, wv, wo, wd, aup):
     f32, bf16 = jnp.float32, jnp.bfloat16
     V = pltpu.VMEM
     D = pltpu.SemaphoreType.DMA
-    n = len(ROUNDS)
     vm = pl.BlockSpec(memory_space=pltpu.VMEM)
     hb = pl.BlockSpec(memory_space=pl.ANY)
-    loss, gdown, gup = pl.pallas_call(
+    packed = pl.pallas_call(
         kernel,
         name="dpo_step",
-        out_shape=(
-            jax.ShapeDtypeStruct((8, 128), f32),
-            jax.ShapeDtypeStruct((64, 64), f32),
-            jax.ShapeDtypeStruct((64, 128), f32),
-        ),
+        out_shape=jax.ShapeDtypeStruct((136, 128), f32),
         in_specs=[hb, hb, pl.BlockSpec(memory_space=pltpu.SMEM)] + [vm] * 7,
-        out_specs=(vm, vm, vm),
+        out_specs=vm,
         scratch_shapes=[
             V((128, 8192), bf16), V((128, 8192), bf16), V((128, 8192), bf16),
             V((32, 1152, 128), bf16), V((8, 128, 128), f32), V((3, 2, 256, 128), bf16), V((2, 64, 256), bf16),
@@ -473,7 +510,7 @@
             V((64, 128), f32), V((64, 128), f32), V((40, 128), f32), V((4, 40, 128), f32), V((40, 128), f32),
             V((8, 40, 128), f32), V((40, 128), f32), V((8, 40, 128), f32), V((40, 128), f32), V((40, 128), f32), V((32, 128), f32), V((32, 128), f32),
             V((4, 128, 128), f32),
-            D((2,)), D((n, 6)), D((n, 6)), D((n, 6)), D((n, 6)), D((4,)), D((4,)), D((4,)), D((4,)), D((4,)), D((4,)),
+            D((2,)), D((1,)), D((SENDS,)), D((1,)), D((8,)), D((4,)), D((4,)), D((4,)), D((4,)), D((4,)), D((4,)),
             D((4,)), D((4,)), D((8,)), D((8,)), D((8,)), D((8,)), D((8,)), D((8,)), D((8,)), D((8,)), D((4,)), D((4,)),
             D((1,)), D((1,)), D((1,)), D((1,)), D((4,)), D((4,)), D((8,)), D((8,)), D((8,)), D((8,)), D((1,)), D((1,)),
         ],
@@ -481,10 +518,20 @@
             collective_id=0, has_side_effects=True, vmem_limit_bytes=56 * 2**20
         ),
     )(
-        x_in.reshape(128, 8192), t_in.reshape(128, 8192), rlen, scale.reshape(1, 8192), wq, wk, wv, wo, wd, aup
+        x_in.reshape(128, 8192), t_in.reshape(128, 8192), rlen, scale.reshape(1, 8192), wq, wk, wv, wo, wd.T, aup
     )
-    return loss[0, 0], gdown, gup
-
+    loss, gdown, gup = pl.pallas_call(
+        split,
+        name="split",
+        out_shape=(
+            jax.ShapeDtypeStruct((1, 1), f32),
+            jax.ShapeDtypeStruct((64, 64), f32),
+            jax.ShapeDtypeStruct((64, 128), f32),
+        ),
+        in_specs=[vm],
+        out_specs=(pl.BlockSpec(memory_space=pltpu.SMEM), vm, vm),
+    )(packed)
+    return loss.reshape(()), gdown, gup
 
 def solution(mesh):
     return jax.shard_map(

time: 104 us -> 88.1 us (0.85)
  Pallas kernels: 98 us -> 87.2 us
  local copies, waits for them, and re-layouts: 5.42 us -> 0 us
    pallas_call x1 -> x2, Pallas kernels: 98 us -> 87.2 us  [the longest x1 85.7 us: step(): pl.pallas_call(kernel, name='dpo_step', out_shape=jax.ShapeDtypeStruct((1...]
    unnamed x3 -> x0, local copies, waits for them, and re-layouts: 4.23 us -> none
    slice x1 -> x0, local copies, waits for them, and re-layouts: 1.2 us -> none  [step(): return (loss[0, 0], gdown, gup)]
where the time goes in v2:
time: 88.1 us; the launch traced here: 87.9 us
  Pallas kernels  87.2 us (99%)
    pallas_call x1, Pallas kernels, step(): pl.pallas_call(kernel, name='dpo_step', out_shape=jax.ShapeDtypeStruct((1...  85.7 us

profile of v2, /device:TPU:1, one launch (start us, length us, event | category | flops | bytes accessed | tf_op | source)
XLA Modules:
  0.0 87.9 jit_solution(790507719606961186)
XLA Ops:
  0.6 85.7 %dpo_step.1.packed = f32[136,128]{1,0:T(8,128)} custom-call(bf16[128,8192]{1,0:T(8,128)(2,1)} %bitcast.5, bf16[128,8192]{1,0:T(8,128)(2,1)} %bitcast.6, s32[2]{0:T(128)} %rlen.1, f32[1,8192]{1,0:T(1,128)} %bitcast.7, bf16[256,128]{1,0:T(8,128)(2,1)} %wq.1, bf16[256,128]{1,0:T(8,128)(2,1)} %wk.1, bf16[256,128]{1,0:T(8,128)(2,1)} %wv.1, bf16[256,128]{1,0:T(8,128)(2,1)} %wo.1, ...), custom_call_target="tpu_custom_call" | custom-call | tf_op jit(solution)/shard_map/dpo_step/pallas_call | solution.py:496
  86.4 1.5 %split.1 = (f32[1,1]{1,0:T(1,128)}, f32[64,64]{1,0:T(8,128)}, f32[64,128]{1,0:T(8,128)}) custom-call(f32[136,128]{1,0:T(8,128)} %dpo_step.1.packed), custom_call_target="tpu_custom_call" | custom-call | tf_op jit(solution)/shard_map/split/pallas_call | solution.py:523

commit v3 on v2

--- a/solution.py
+++ b/solution.py
@@ -20,28 +20,28 @@
     (1,3), (0,2,7,0,0,0), (1,7), (0,5,0,1,1,1), (0,2,0,1,1,0), (0,4,1,0,0,1), (1,6), (0,3,1,0,1,0), (1,11),
     (0,5,0,1,0,0), (1,9), (0,3,1,0,1,1), (1,10), (0,2,7,0,1,0), (1,8), (0,4,7,0,0,1), (1,15), (0,5,1,1,0,0), (1,13),
     (0,0,6,0,1,1), (0,1,1,1,0,0), (0,2,6,0,1,1), (1,14), (0,3,2,0,0,0), (1,12), (0,4,0,2,1,0), (1,18), (0,5,7,1,1,1),
-    (1,19), (0,2,6,0,0,0), (1,17), (0,3,2,0,0,1), (1,16), (0,4,0,2,0,1), (1,21), (0,5,7,1,1,0), (1,22),
+    (1,19), (0,2,6,0,0,0), (1,17), (0,3,2,0,0,1), (1,16), (0,4,0,2,0,1), (1,21), (0,5,7,1,1,0), (3,0,1,4,28), (1,22),
     (0,1,1,1,0,1), (0,0,7,1,1,0), (0,2,7,1,1,0), (1,23), (0,4,2,0,1,0), (1,20), (0,3,0,2,1,1), (1,27), (0,5,7,1,0,1),
-    (3,0,1,4,28), (0,2,7,1,0,1), (0,3,1,1,0,1), (0,4,0,2,1,1), (1,28), (0,0,1,2,0,0), (0,5,1,1,0,1), (1,33),
-    (0,1,0,3,1,0), (0,2,0,3,1,0), (0,3,1,2,0,0), (0,4,1,2,0,0), (1,24), (1,25), (1,26), (1,31), (0,0,5,0,1,1),
-    (1,36), (0,1,3,0,0,1), (1,37), (0,3,0,3,0,1), (1,34), (0,2,7,2,1,1), (0,4,7,2,1,1), (1,29), (1,30), (1,32),
-    (1,40), (0,5,7,1,0,0), (1,35), (0,0,5,0,0,0), (0,1,3,0,0,0), (1,41), (0,2,6,1,1,0), (1,43), (0,3,1,2,1,1),
-    (0,4,3,0,0,0), (0,5,6,1,1,0), (0,0,6,1,1,0), (1,46), (0,1,2,1,0,1), (0,2,5,0,1,1), (0,4,5,0,1,1), (0,3,0,3,1,0),
-    (1,38), (1,39), (1,42), (1,45), (0,0,6,1,0,1), (0,5,6,1,0,1), (1,51), (0,1,7,3,1,0), (0,2,7,3,1,0),
-    (0,4,3,0,0,1), (1,52), (0,3,2,2,0,0), (1,44), (1,47), (0,0,2,2,0,0), (0,5,2,1,0,1), (1,56), (0,1,1,3,0,1),
-    (0,3,1,3,0,1), (1,58), (0,2,7,3,1,1), (0,4,2,2,0,0), (1,48), (1,49), (1,50), (1,53), (0,5,2,2,0,0),
-    (3,2,8,24,29), (0,0,7,3,1,1), (1,62), (0,1,5,1,1,0), (1,55), (0,4,3,0,1,1), (1,63), (0,3,2,2,1,1), (0,2,5,1,1,0),
-    (1,54), (1,57), (1,65), (0,0,6,2,1,0), (0,5,5,1,1,0), (1,68), (0,1,4,0,1,1), (0,4,2,2,1,1), (0,2,6,2,1,1),
-    (0,3,3,0,0,0), (1,59), (1,60), (1,61), (1,64), (1,69), (0,0,5,1,1,1), (1,75), (0,5,3,1,0,1), (1,76),
-    (0,1,3,2,0,0), (0,4,3,2,0,0), (1,74), (0,2,6,3,1,0), (0,3,3,2,0,0), (1,66), (1,67), (1,70), (0,0,6,3,1,0),
-    (1,81), (0,1,6,3,1,1), (0,4,4,0,1,1), (0,2,6,3,1,1), (1,80), (0,3,2,3,0,1), (1,71), (1,72), (1,73), (1,85),
-    (0,5,5,1,0,0), (1,82), (0,0,2,3,0,0), (1,88), (0,1,4,1,1,0), (1,87), (0,4,3,2,1,1), (0,2,6,2,0,1), (0,3,3,2,1,1),
-    (1,77), (1,78), (1,79), (0,5,4,1,1,0), (0,0,3,1,0,0), (1,94), (0,1,4,0,0,0), (1,91), (0,4,4,0,0,1), (1,83),
-    (1,84), (1,86), (1,96), (0,3,3,2,0,1), (3,3,5,6,12,20,30), (1,99), (0,2,5,3,1,0), (0,0,5,3,1,0), (1,98),
-    (0,1,3,3,0,0), (1,100), (0,4,4,2,0,0), (1,89), (1,90), (1,92), (1,93), (1,105), (0,3,3,3,0,1), (1,104),
-    (0,0,5,3,1,1), (0,2,5,3,1,1), (1,95), (1,97), (1,101), (1,102), (1,103), (1,106), (1,107), (1,108), (1,109),
-    (1,110), (1,111), (1,112), (1,113), (1,114), (1,115), (1,116), (1,117), (1,118), (1,119), (1,120), (1,121),
-    (1,122), (1,123), (3,7,9,10,11,13,14,15,16,17,18,19,21,22,23,25,26,27,31),
+    (0,2,7,1,0,1), (0,3,1,1,0,1), (0,4,0,2,1,1), (1,28), (0,0,1,2,0,0), (0,5,1,1,0,1), (1,33), (0,1,0,3,1,0),
+    (0,2,0,3,1,0), (0,3,1,2,0,0), (0,4,1,2,0,0), (1,24), (1,25), (1,26), (1,31), (0,0,5,0,1,1), (1,36),
+    (0,1,3,0,0,1), (1,37), (0,3,0,3,0,1), (1,34), (0,2,7,2,1,1), (0,4,7,2,1,1), (1,29), (1,30), (1,32), (1,40),
+    (0,5,7,1,0,0), (1,35), (0,0,5,0,0,0), (0,1,3,0,0,0), (1,41), (0,2,6,1,1,0), (1,43), (0,3,1,2,1,1), (0,4,3,0,0,0),
+    (0,5,6,1,1,0), (0,0,6,1,1,0), (1,46), (0,1,2,1,0,1), (0,2,5,0,1,1), (0,4,5,0,1,1), (0,3,0,3,1,0), (1,38), (1,39),
+    (1,42), (1,45), (0,0,6,1,0,1), (0,5,6,1,0,1), (1,51), (0,1,7,3,1,0), (0,2,7,3,1,0), (0,4,3,0,0,1), (1,52),
+    (0,3,2,2,0,0), (1,44), (1,47), (0,0,2,2,0,0), (3,2,8,24,29), (0,5,2,1,0,1), (1,56), (0,1,1,3,0,1), (0,3,1,3,0,1),
+    (1,58), (0,2,7,3,1,1), (0,4,2,2,0,0), (1,48), (1,49), (1,50), (1,53), (0,5,2,2,0,0), (0,0,7,3,1,1), (1,62),
+    (0,1,5,1,1,0), (1,55), (0,4,3,0,1,1), (1,63), (0,3,2,2,1,1), (0,2,5,1,1,0), (1,54), (1,57), (1,65),
+    (0,0,6,2,1,0), (0,5,5,1,1,0), (1,68), (0,1,4,0,1,1), (0,4,2,2,1,1), (0,2,6,2,1,1), (0,3,3,0,0,0), (1,59), (1,60),
+    (1,61), (1,64), (1,69), (0,0,5,1,1,1), (1,75), (0,5,3,1,0,1), (1,76), (0,1,3,2,0,0), (0,4,3,2,0,0), (1,74),
+    (0,2,6,3,1,0), (0,3,3,2,0,0), (1,66), (1,67), (1,70), (0,0,6,3,1,0), (1,81), (0,1,6,3,1,1), (0,4,4,0,1,1),
+    (0,2,6,3,1,1), (1,80), (0,3,2,3,0,1), (1,71), (1,72), (1,73), (1,85), (0,5,5,1,0,0), (1,82), (0,0,2,3,0,0),
+    (1,88), (0,1,4,1,1,0), (1,87), (0,4,3,2,1,1), (0,2,6,2,0,1), (0,3,3,2,1,1), (1,77), (1,78), (1,79),
+    (0,5,4,1,1,0), (3,3,5,6,12,20,30), (0,0,3,1,0,0), (1,94), (0,1,4,0,0,0), (1,91), (0,4,4,0,0,1), (1,83), (1,84),
+    (1,86), (1,96), (0,3,3,2,0,1), (1,99), (0,2,5,3,1,0), (0,0,5,3,1,0), (1,98), (0,1,3,3,0,0), (1,100),
+    (0,4,4,2,0,0), (1,89), (1,90), (1,92), (1,93), (1,105), (0,3,3,3,0,1), (1,104), (0,0,5,3,1,1), (0,2,5,3,1,1),
+    (1,95), (1,97), (1,101), (1,102), (1,103), (1,106), (1,107), (1,108), (1,109), (1,110), (1,111), (1,112),
+    (3,7,9,10,14,21,25,31), (1,113), (1,114), (1,115), (1,116), (1,117), (1,118), (1,119), (1,120), (1,121),
+    (3,11,22,26,27), (1,122), (1,123), (3,13,15,16,17,18,19,23),
 )
 
 def arrives(way, piece):
@@ -63,14 +63,14 @@
     return lax.dot_general(a, b, (((ca,), (cb,)), ((), ())), preferred_element_type=jnp.float32)
 
 def kernel(
-    x_hbm, t_hbm, rlen, scale, wq, wk, wv, wo, wd, aup,
+    x_hbm, t_hbm, rlen, scale_hbm, wq, wk, wv, wo, wd, aup_hbm,
     out_ref,
-    xs, ts, nx, W, acc, kv, att, vgs, vgr, vgo, mgs, mgr,
+    xs, ts, scale, aup, nx, W, acc, kv, att, vgs, vgr, vgo, mgs, mgr,
     dkeep, dsend, drecv, s1, r1y, r1z, s2y, s2z, r2y, r2z, s3, r3, s4, r4,
-    us, ur, uxs, uxr, uys, uyr, uzs, uzr, ucs, ucr, ues, uer, stat,
+    us, uxs, uxr, uys, uyr, uzs, uzr, ucs, ucr, uas, uer, stat,
     in_sem, ag_s, ag_r, cc_s, cc_r, kv_s, kv_r, vg_s, vg_r, mg_s, mg_r, dc_s, dc_r,
     y1_s, y1_r, z1_s, z1_r, y2_s, y2_r, z2_s, z2_r, x3_s, x3_r, c4_s, c4_r,
-    uc_s, uc_r, ux_s, ux_r, uy_s, uy_r, uz_s, uz_r, ue_s, ue_r,
+    uc_s, uc_r, ux_s, ux_r, uy_s, uy_r, uz_s, uz_r, ue_s, ue_r, ua_s, ua_r,
 ):
     f32, bf16 = jnp.float32, jnp.bfloat16
     dp, f, x = lax.axis_index("dp"), lax.axis_index("fsdp"), lax.axis_index("seq")
@@ -97,14 +97,26 @@
 
     in_x = pltpu.make_async_copy(x_hbm, xs, in_sem.at[0])
     in_t = pltpu.make_async_copy(t_hbm, ts, in_sem.at[1])
+
+    own_in = [
+        pltpu.make_async_copy(w, W.at[f, pl.ds(k * 288, 256), :], in_sem.at[2 + k])
+        for k, w in enumerate((wq, wk, wv, wo))
+    ]
+    own_in += [
+        pltpu.make_async_copy(
+            wd.at[pl.ds((k % 2) * 32, 32), pl.ds((k // 2) * 128, 128)],
+            W.at[f, pl.ds(k * 288 + 256, 32), :],
+            in_sem.at[6 + k],
+        )
+        for k in range(4)
+    ]
+    in_scale = pltpu.make_async_copy(scale_hbm, scale, in_sem.at[10])
+    in_aup = pltpu.make_async_copy(aup_hbm, aup, in_sem.at[11])
+    for cp in own_in + [in_scale, in_aup]:
+        cp.start()
     in_x.start()
     in_t.start()
-
-    for k, w in enumerate((wq, wk, wv, wo)):
-        W[f, k * 288 : k * 288 + 256, :] = w[...]
-        W[f, k * 288 + 256 : k * 288 + 288, :] = wd[(k % 2) * 32 : (k % 2) * 32 + 32, (k // 2) * 128 : (k // 2) * 128 + 128]
     kv[...] = jnp.zeros_like(kv)
-    acc[...] = jnp.zeros_like(acc)
 
     barrier = pltpu.get_barrier_semaphore()
     greet = [sib]
@@ -115,6 +127,9 @@
     greet += [dev(x, (y + o) % 8, other, c) for o in range(1, 8)]
     for to in greet:
         pl.semaphore_signal(barrier, inc=1, device_id=to)
+    acc[...] = jnp.zeros_like(acc)
+    for cp in own_in + [in_scale, in_aup]:
+        cp.wait()
     pl.semaphore_wait(barrier, len(greet))
 
     pairs = [h, (h + 3 + 2 * zl) % 4, (h + 1 + 2 * (1 - zl) * 0 + 2 * zl) % 4, (h + 2) % 4]
@@ -358,9 +373,13 @@
         dcs.append(cp)
 
     uc.wait()
-    uxs[0:32, :] = us[keep, :] + ucr[0:32, :]
-    uxs[32:40, :] = loss + ucr[32:40, :]
-    uxc = [remote(uxs, uxr.at[o], ux_s.at[o], ux_r.at[o], dev((x + o) % 4, y, z, c)) for o in range(4)]
+    uxs[...] = us[keep, :] + ucr[0:32, :]
+    uys[8:16, :] = loss + ucr[32:40, :]
+    uxc = []
+    for o in range(4):
+        tx = (x + o) % 4
+        src = uxs.at[pl.ds(pl.multiple_of(tx * 8, 8), 8), :]
+        uxc.append(remote(src, uxr.at[o], ux_s.at[o], ux_r.at[o], dev(tx, y, z, c)))
     for o in (1, 2, 3):
         uxc[o].start()
 
@@ -379,7 +398,8 @@
         z1[o].start()
     for o in (1, 2, 3):
         uxc[o].wait()
-    uys[...] = uxs[...] + uxr[1] + uxr[2] + uxr[3]
+    eighth = pl.ds(pl.multiple_of(x * 8, 8), 8)
+    uys[0:8, :] = uxs[eighth, :] + uxr[1] + uxr[2] + uxr[3]
     uyc = [remote(uys, uyr.at[o], uy_s.at[o], uy_r.at[o], dev(x, (y + o) % 8, z, c)) for o in range(8)]
     for o in range(1, 8):
         uyc[o].start()
@@ -452,19 +472,25 @@
     tot = uzs[...]
     for o in range(1, 8):
         tot += uzr[o]
-    ues[...] = tot[0:32, :]
-    ue = remote(ues, uer, ue_s.at[0], ue_r.at[0], sib)
-    ue.start()
-    out_ref[128:136, :] = tot[32:40, :] * (1.0 / 512.0)
+    uas[eighth, :] = tot[0:8, :]
+    uac = []
+    for o in range(4):
+        ref = uas.at[eighth, :]
+        uac.append(remote(ref, ref, ua_s.at[o], ua_r.at[o], dev((x + o) % 4, y, z, c)))
+    for o in (1, 2, 3):
+        uac[o].start()
+    out_ref[128:136, :] = tot[8:16, :] * (1.0 / 128.0)
     for o in (1, 2, 3):
         x3[o].wait()
     mine = s3[x // 2] + r3[1] + r3[2] + r3[3]
     s4[...] = mine
     c4 = remote(s4, r4, c4_s.at[0], c4_r.at[0], sib)
     c4.start()
-    ue.wait()
-    out_ref[keep, :] = ues[...]
-    out_ref[give, :] = uer[...]
+    for o in (1, 2, 3):
+        uac[o].wait()
+    ue = remote(uas, uer, ue_s.at[0], ue_r.at[0], sib)
+    ue.start()
+    out_ref[keep, :] = uas[...]
     for o in (1, 2, 3):
         @pl.when(x + o < 4)
         def _():
@@ -475,6 +501,8 @@
     for n in range(4):
         dcs[n].wait_send()
     c4.wait()
+    ue.wait()
+    out_ref[give, :] = uer[...]
     low = jnp.where(c == 0, s4[...], r4[...])
     high = jnp.where(c == 0, r4[...], s4[...])
     whole = jnp.concatenate([low, high], axis=0)
@@ -497,22 +525,22 @@
         kernel,
         name="dpo_step",
         out_shape=jax.ShapeDtypeStruct((136, 128), f32),
-        in_specs=[hb, hb, pl.BlockSpec(memory_space=pltpu.SMEM)] + [vm] * 7,
+        in_specs=[hb, hb, pl.BlockSpec(memory_space=pltpu.SMEM)] + [hb] * 7,
         out_specs=vm,
         scratch_shapes=[
-            V((128, 8192), bf16), V((128, 8192), bf16), V((128, 8192), bf16),
+            V((128, 8192), bf16), V((128, 8192), bf16), V((1, 8192), f32), V((64, 128), bf16), V((128, 8192), bf16),
             V((32, 1152, 128), bf16), V((8, 128, 128), f32), V((3, 2, 256, 128), bf16), V((2, 64, 256), bf16),
             V((2, 256, 128), bf16), V((4, 2, 64, 128), bf16), V((2, 256, 128), f32), V((8, 128), f32), V((4, 8, 128), f32),
             V((32, 32, 256), f32), V((32, 32, 256), bf16), V((32, 32, 256), bf16), V((4, 8, 32, 256), bf16),
             V((8, 4, 16, 256), bf16), V((8, 4, 16, 256), bf16), V((4, 16, 256), bf16), V((4, 16, 256), bf16),
             V((8, 16, 256), bf16), V((8, 16, 256), bf16), V((2, 32, 128), f32), V((4, 32, 128), f32),
             V((32, 128), f32), V((32, 128), f32),
-            V((64, 128), f32), V((64, 128), f32), V((40, 128), f32), V((4, 40, 128), f32), V((40, 128), f32),
-            V((8, 40, 128), f32), V((40, 128), f32), V((8, 40, 128), f32), V((40, 128), f32), V((40, 128), f32), V((32, 128), f32), V((32, 128), f32),
+            V((64, 128), f32), V((32, 128), f32), V((4, 8, 128), f32), V((16, 128), f32), V((8, 16, 128), f32),
+            V((16, 128), f32), V((8, 16, 128), f32), V((40, 128), f32), V((40, 128), f32), V((32, 128), f32), V((32, 128), f32),
             V((4, 128, 128), f32),
-            D((2,)), D((1,)), D((SENDS,)), D((1,)), D((8,)), D((4,)), D((4,)), D((4,)), D((4,)), D((4,)), D((4,)),
+            D((12,)), D((1,)), D((SENDS,)), D((1,)), D((8,)), D((4,)), D((4,)), D((4,)), D((4,)), D((4,)), D((4,)),
             D((4,)), D((4,)), D((8,)), D((8,)), D((8,)), D((8,)), D((8,)), D((8,)), D((8,)), D((8,)), D((4,)), D((4,)),
-            D((1,)), D((1,)), D((1,)), D((1,)), D((4,)), D((4,)), D((8,)), D((8,)), D((8,)), D((8,)), D((1,)), D((1,)),
+            D((1,)), D((1,)), D((1,)), D((1,)), D((4,)), D((4,)), D((8,)), D((8,)), D((8,)), D((8,)), D((1,)), D((1,)), D((4,)), D((4,)),
         ],
         compiler_params=pltpu.CompilerParams(
             collective_id=0, has_side_effects=True, vmem_limit_bytes=56 * 2**20

time: 88.1 us -> 85.5 us (0.970)
  Pallas kernels: 87.2 us -> 84.6 us
    pallas_call x1, Pallas kernels: 85.7 us -> 83.1 us  [step(): pl.pallas_call(kernel, name='dpo_step', out_shape=jax.ShapeDtypeStruct((1...]
where the time goes in v3:
time: 85.5 us; the launch traced here: 85.3 us
  Pallas kernels  84.6 us (99%)
    pallas_call x1, Pallas kernels, step(): pl.pallas_call(kernel, name='dpo_step', out_shape=jax.ShapeDtypeStruct((1...  83.1 us

profile of v3, /device:TPU:1, one launch (start us, length us, event | category | flops | bytes accessed | tf_op | source)
XLA Modules:
  0.0 85.3 jit_solution(15323702802674376436)
XLA Ops:
  0.6 83.1 %dpo_step.1.packed = f32[136,128]{1,0:T(8,128)} custom-call(bf16[128,8192]{1,0:T(8,128)(2,1)} %bitcast.5, bf16[128,8192]{1,0:T(8,128)(2,1)} %bitcast.6, s32[2]{0:T(128)} %rlen.1, f32[1,8192]{1,0:T(1,128)} %bitcast.7, bf16[256,128]{1,0:T(8,128)(2,1)} %wq.1, bf16[256,128]{1,0:T(8,128)(2,1)} %wk.1, bf16[256,128]{1,0:T(8,128)(2,1)} %wv.1, bf16[256,128]{1,0:T(8,128)(2,1)} %wo.1, ...), custom_call_target="tpu_custom_call" | custom-call | tf_op jit(solution)/shard_map/dpo_step/pallas_call | solution.py:524
  83.8 1.5 %split.1 = (f32[1,1]{1,0:T(1,128)}, f32[64,64]{1,0:T(8,128)}, f32[64,128]{1,0:T(8,128)}) custom-call(f32[136,128]{1,0:T(8,128)} %dpo_step.1.packed), custom_call_target="tpu_custom_call" | custom-call | tf_op jit(solution)/shard_map/split/pallas_call | solution.py:551

commit v4 on v3

--- a/solution.py
+++ b/solution.py
@@ -44,6 +44,7 @@
     (3,11,22,26,27), (1,122), (1,123), (3,13,15,16,17,18,19,23),
 )
 
+
 def arrives(way, piece):
     dy, pair, half, part = piece
     if way < 2:
@@ -56,11 +57,14 @@
         return (dy, (1, 0, 3, 2)[pair], half, part)
     return (dy, (0, 2, 1, 3)[pair], half, part)
 
+
 def dot(a, b):
     return jnp.dot(a, b, preferred_element_type=jnp.float32)
 
+
 def dot_general(a, b, ca, cb):
     return lax.dot_general(a, b, (((ca,), (cb,)), ((), ())), preferred_element_type=jnp.float32)
+
 
 def kernel(
     x_hbm, t_hbm, rlen, scale_hbm, wq, wk, wv, wo, wd, aup_hbm,
@@ -132,6 +136,7 @@
         cp.wait()
     pl.semaphore_wait(barrier, len(greet))
 
+
     pairs = [h, (h + 3 + 2 * zl) % 4, (h + 1 + 2 * (1 - zl) * 0 + 2 * zl) % 4, (h + 2) % 4]
     pairs[1] = (h + 3 + 2 * zl) % 4
     pairs[2] = (h + 1 + 2 * zl) % 4
@@ -210,9 +215,8 @@
             for k, block in enumerate(blocks):
                 g += jnp.where(i == k, 1, 0) * (pairs[block % 4] * 8 + (y + block // 4) % 8)
             cols = pl.ds(pl.multiple_of(g * 256, 256), 256)
-            a, raw, tgt = nx[:, cols], xs[:, cols], ts[:, cols]
+            a = nx[:, cols]
             qk = jnp.concatenate([W[g, 0:256, :], W[g, 288:544, :]], axis=1)
-            out = W[g, 864:1120, :]
             down = jnp.concatenate(
                 [jnp.concatenate([W[g, 288 * k + 256 : 288 * k + 288, :] for k in (k0, k0 + 1)], axis=0) for k0 in (0, 2)],
                 axis=1,
@@ -222,12 +226,17 @@
             acc[1] += both[:, 128:256]
             acc[2] += dot(a, W[g, 576:832, :])
             acc[3, :, 0:64] += dot_general(a, down, 1, 1)
-            acc[5] += dot(raw, out)
-            acc[6] += dot(tgt, out)
-            acc[7] += dot_general(out, out, 0, 0)
             return carry
 
         lax.fori_loop(0, len(blocks), body, 0, unroll=2)
+
+    def multiply_out(g, carry):
+        cols = pl.ds(pl.multiple_of(g * 256, 256), 256)
+        out = W[g, 864:1120, :]
+        acc[5] += dot(xs[:, cols], out)
+        acc[6] += dot(ts[:, cols], out)
+        acc[7] += dot_general(out, out, 0, 0)
+        return carry
 
     n = 0
     for do in GATHER:
@@ -240,6 +249,7 @@
             norm_rows()
         else:
             multiply(do[1:])
+
 
     def rope(v):
         return (v * stat[2] + pltpu.roll(v, 64, 1) * stat[3]).astype(bf16)
@@ -274,6 +284,7 @@
             def _():
                 vgc[o].wait_send()
 
+    lax.fori_loop(0, 32, multiply_out, 0, unroll=2)
     g_hi = acc[7].astype(bf16)
     g_lo = (acc[7] - g_hi.astype(f32)).astype(bf16)
     whole(31, ag_s.at[0]).wait()
@@ -282,6 +293,7 @@
         @pl.when(x - o >= 0)
         def _():
             kvs[o].wait_recv()
+
 
     row = lax.broadcasted_iota(jnp.int32, (64, 256), 0)
     col = lax.broadcasted_iota(jnp.int32, (64, 256), 1)
@@ -348,6 +360,7 @@
             vgo[0, 0:128, :] += vgr[o].reshape(128, 128).astype(f32)
     vg = (vgo[0, 0:128, :] * pull[0:1, :]).astype(bf16)
 
+
     up = dot_general(d_in, vg, 0, 0)
     agt = dot_general(aup[...], vg, 1, 1).astype(bf16)
 
@@ -387,6 +400,7 @@
         dcs[n].wait_recv()
         s1[n] = (dkeep[n * 8 : n * 8 + 8] + drecv[n * 8 : n * 8 + 8].astype(f32)).astype(bf16)
 
+
     y1, z1 = [], []
     for o in range(8):
         ty, tz = (y + o) % 8, (z + o) % 8
@@ -414,6 +428,7 @@
     s2y[...] = sy.astype(bf16)
     s2z[...] = sz.astype(bf16)
 
+
     y2 = []
     for o in range(8):
         tz = (z + o) % 8
@@ -460,6 +475,7 @@
     for k in range(2):
         s3[k, 0:16, :] = ty_[:, k * 128 : k * 128 + 128]
         s3[k, 16:32, :] = tz_[:, k * 128 : k * 128 + 128]
+
 
     x3 = []
     for o in range(4):
@@ -510,10 +526,12 @@
     out_ref[64:128, 0:64] = whole.T[0:64, :]
     out_ref[64:128, 64:128] = jnp.zeros((64, 64), f32)
 
+
 def split(packed, loss_ref, gdown_ref, gup_ref):
     loss_ref[0, 0] = jnp.max(packed[128:136, :])
     gdown_ref[...] = packed[64:128, 0:64]
     gup_ref[...] = packed[0:64, :]
+
 
 def step(x_in, t_in, rlen, scale, wq, wk, wv, wo, wd, aup):
     f32, bf16 = jnp.float32, jnp.bfloat16
@@ -561,6 +579,7 @@
     )(packed)
     return loss.reshape(()), gdown, gup
 
+
 def solution(mesh):
     return jax.shard_map(
         step,

time: 85.5 us -> 84.5 us (0.988)
  Pallas kernels: 84.6 us -> 83.7 us
    pallas_call x1, Pallas kernels: 83.1 us -> 82.2 us  [step(): pl.pallas_call(kernel, name='dpo_step', out_shape=jax.ShapeDtypeStruct((1...]
where the time goes in v4:
time: 84.5 us; the launch traced here: 84.4 us
  Pallas kernels  83.7 us (99%)
    pallas_call x1, Pallas kernels, step(): pl.pallas_call(kernel, name='dpo_step', out_shape=jax.ShapeDtypeStruct((1...  82.2 us

profile of v4, /device:TPU:1, one launch (start us, length us, event | category | flops | bytes accessed | tf_op | source)
XLA Modules:
  0.0 84.4 jit_solution(4222224037918849228)
XLA Ops:
  0.6 82.2 %dpo_step.1.packed = f32[136,128]{1,0:T(8,128)} custom-call(bf16[128,8192]{1,0:T(8,128)(2,1)} %bitcast.5, bf16[128,8192]{1,0:T(8,128)(2,1)} %bitcast.6, s32[2]{0:T(128)} %rlen.1, f32[1,8192]{1,0:T(1,128)} %bitcast.7, bf16[256,128]{1,0:T(8,128)(2,1)} %wq.1, bf16[256,128]{1,0:T(8,128)(2,1)} %wk.1, bf16[256,128]{1,0:T(8,128)(2,1)} %wv.1, bf16[256,128]{1,0:T(8,128)(2,1)} %wo.1, ...), custom_call_target="tpu_custom_call" | custom-call | tf_op jit(solution)/shard_map/dpo_step/pallas_call | solution.py:542
  82.8 1.5 %split.1 = (f32[1,1]{1,0:T(1,128)}, f32[64,64]{1,0:T(8,128)}, f32[64,128]{1,0:T(8,128)}) custom-call(f32[136,128]{1,0:T(8,128)} %dpo_step.1.packed), custom_call_target="tpu_custom_call" | custom-call | tf_op jit(solution)/shard_map/split/pallas_call | solution.py:569
